TPU v7x, 256 devices: a whole 4x4x8 slice. The times are simulated.
256 devices in a mesh: wide: 64 (over y, z, core), narrow: 4 (over x).
Axes of the slice: x: 4, y: 4, z: 8, core: 2. Of those that a mesh axis runs over, the one named last changes fastest.
Arguments:
- tensor_blocks: bfloat16 [6144, 64, 4096], P(('wide', 'narrow')), may hold values from -6 to 6
- block_rows: int32 [6144], P(('wide', 'narrow')), may hold values from 0 to 255, as said below
- block_seconds: int32 [6144], P(('wide', 'narrow')), may hold values from 0 to 511, as said below
- block_thirds: int32 [6144], P(('wide', 'narrow')), may hold values from 0 to 127, as said below
- second_factor: bfloat16 [32768, 256], P('wide')
- third_factor: bfloat16 [8192, 256], P('wide')
Outputs:
- new_factor: float32 [16384, 256], P(('wide', 'narrow'))
Inputs may be any that keep to these rules, and one draw needn't show every extreme that they name: `block_rows`: blocks d * 24 to (d + 1) * 24 - 1 lie on device d of wide+narrow; their mode-1 row blocks lie in w * 4 to (w + 1) * 4 - 1, w being the device's index along wide. `block_seconds`: row block j of second_factor is held by index j // 8 of wide. Among the blocks of all devices of one index of wide together, at most 4 name row blocks held by one index of wide; in every draw one index of wide, the same for all, is named by exactly 4 blocks of every index of wide. `block_thirds`: row block k of third_factor is held by index k // 2 of wide. Among the blocks of all devices of one index of wide together, at most 4 name row blocks held by one index of wide; in every draw one index of wide, the same for all, is named by exactly 4 blocks of every index of wide.
All inputs are finite; a program needn't handle non-finite values.
Results may differ from a plain program's by a relative error of at most 0.0034.
Values may be sent and summed in bfloat16 or wider, within the bound.
No kernel may reach another device: no remote copies, remote signals or barrier semaphores. Data moves between devices by JAX's collectives and lax.ppermute only.
A program may use at most 128 MiB of HBM per device.

v0:
```python
import jax
import jax.numpy as jnp
from jax import lax
from jax.sharding import PartitionSpec as P

BS = 64
R = 256
R1_DEV = 4


def fetch_plan(identity, per_holder, holders, places_each):
    holder = identity // per_holder
    within = identity - holder * per_holder
    serial = jnp.arange(identity.shape[0])
    earlier = (holder[:, None] == holder[None, :]) & (serial[None, :] < serial[:, None])
    placed = jnp.sum(earlier.astype(jnp.int32), axis=1)
    requests = jnp.zeros((holders, places_each), jnp.int32).at[holder, placed].set(within)
    return (requests, holder * places_each + placed)


def body(tensor_blocks, block_rows, block_seconds, block_thirds, second_factor, third_factor):
    holders = lax.axis_size("wide")
    parts_narrow = lax.axis_size("narrow")
    narrow_at = lax.axis_index("narrow")
    blocks_here = tensor_blocks.shape[0]
    pooled = blocks_here * parts_narrow
    base_cap = max(2, -(-pooled // holders))
    places_each = -(-base_cap // parts_narrow) * parts_narrow
    slots_mine = places_each // parts_narrow
    own_second = second_factor.reshape(-1, BS, R)
    own_third = third_factor.reshape(-1, BS, R)
    group_names = lax.all_gather(block_seconds, "narrow", axis=0, tiled=True)
    requests, position = fetch_plan(group_names, own_second.shape[0], holders, places_each)
    mine = lax.dynamic_slice_in_dim(requests, narrow_at * slots_mine, slots_mine, 1)
    replies = jnp.take(
        own_second, lax.all_to_all(mine, "wide", split_axis=0, concat_axis=0, tiled=True), axis=0
    )
    fetched = lax.all_to_all(replies, "wide", split_axis=0, concat_axis=0, tiled=True)
    spread = lax.all_gather(fetched, "narrow", axis=1, tiled=True)
    wanted = lax.dynamic_slice_in_dim(position, narrow_at * blocks_here, blocks_here, 0)
    second_blocks = jnp.take(spread.reshape(-1, BS, R), wanted, axis=0)
    group_names = lax.all_gather(block_thirds, "narrow", axis=0, tiled=True)
    requests, position = fetch_plan(group_names, own_third.shape[0], holders, places_each)
    mine = lax.dynamic_slice_in_dim(requests, narrow_at * slots_mine, slots_mine, 1)
    replies = jnp.take(
        own_third, lax.all_to_all(mine, "wide", split_axis=0, concat_axis=0, tiled=True), axis=0
    )
    fetched = lax.all_to_all(replies, "wide", split_axis=0, concat_axis=0, tiled=True)
    spread = lax.all_gather(fetched, "narrow", axis=1, tiled=True)
    wanted = lax.dynamic_slice_in_dim(position, narrow_at * blocks_here, blocks_here, 0)
    third_blocks = jnp.take(spread.reshape(-1, BS, R), wanted, axis=0)
    targets = block_rows - lax.axis_index("wide") * R1_DEV

    def one_block(summed, inputs):
        block_data, left_rows, right_rows, target = inputs
        product = (
            left_rows.astype(jnp.float32)[:, None, :] * right_rows.astype(jnp.float32)[None, :, :]
        )
        product = product.reshape(BS * BS, R).astype(jnp.bfloat16)
        contribution = jnp.dot(block_data, product, preferred_element_type=jnp.float32)
        return (summed.at[target].add(contribution), None)

    summed, unused = lax.scan(
        one_block,
        jnp.zeros((R1_DEV, BS, R), jnp.float32),
        (tensor_blocks, second_blocks, third_blocks, targets),
    )
    partial_value = lax.psum_scatter(
        summed.reshape(-1, R), "narrow", scatter_dimension=0, tiled=True
    )

    def gram_share(factor):
        length = factor.shape[0] // parts_narrow
        rows_here = lax.dynamic_slice_in_dim(factor, narrow_at * length, length, 0)
        return lax.dot_general(
            rows_here, rows_here, (((0,), (0,)), ((), ())), preferred_element_type=jnp.float32
        )

    gram_second, gram_third = lax.psum(
        (gram_share(second_factor), gram_share(third_factor)), ("wide", "narrow")
    )
    normal = gram_second * gram_third
    cholesky_factor = jnp.linalg.cholesky(normal)
    halfway = lax.linalg.triangular_solve(
        cholesky_factor, partial_value, left_side=False, lower=True, transpose_a=True
    )
    return lax.linalg.triangular_solve(cholesky_factor, halfway, left_side=False, lower=True)


def solution(mesh):
    in_specs = (
        P(("wide", "narrow"), None, None),
        P(("wide", "narrow")),
        P(("wide", "narrow")),
        P(("wide", "narrow")),
        P("wide", None),
        P("wide", None),
    )
    out_specs = P(("wide", "narrow"), None)
    return jax.shard_map(body, mesh=mesh, in_specs=in_specs, out_specs=out_specs, check_vma=False)
```

profile of v0, /device:TPU:8, one launch (start us, length us, event | category | flops | bytes accessed | tf_op | source)
XLA Modules:
  0.0 629.3 jit_solution(2582068294298859849)
XLA Ops:
  11.2 8.9 %all-reduce.3 = (s32[96]{0:T(128)S(1)}, s32[96]{0:T(128)S(1)}) all-reduce(s32[96]{0:T(128)S(1)} %dynamic-update-slice.14, s32[96]{0:T(128)S(1)} %dynamic-update-slice.15), channel_id=1, replica_groups=mesh['wide'=64,'narrow'=4] {'narrow'}, use_global_device_ids=true, to_apply=%add.1 | all-reduce | flops 192 | bytes 1536
  20.3 5.0 scatter_fusion.1
  25.4 20.5 %all_to_all.29 = s32[64,1,1]{2,1,0:T(1,128)S(1)} all-to-all(s32[64,1,1]{2,1,0:T(1,128)S(1)} %copy.24), channel_id=1, replica_groups=mesh['wide'=64,'narrow'=4] {'wide'}, dimensions={0} | all-to-all | bytes 512 | tf_op jit(solution)/shard_map/all_to_all | solution.py:46
  50.6 5.6 all-to-all-start.3
  58.2 48.2 %all-to-all-done.3 = bf16[64,1,64,256]{3,2,1,0:T(8,128)(2,1)S(1)} async-done(((bf16[64,1,64,256]{3,2,1,0:T(8,128)(2,1)}), bf16[64,1,64,256]{3,2,1,0:T(8,128)(2,1)S(1)}, u32[]{:S(2)}, u32[]{:S(2)}) %all-to-all-start.3) | async-done | bytes 2097184 | tf_op jit(solution)/shard_map/all_to_all | solution.py:48
  108.0 5.0 scatter_fusion
  113.1 16.1 %all_to_all.30 = s32[64,1,1]{2,1,0:T(1,128)S(1)} all-to-all(s32[64,1,1]{2,1,0:T(1,128)S(1)} %copy.23), channel_id=1, replica_groups=mesh['wide'=64,'narrow'=4] {'wide'}, dimensions={0} | all-to-all | bytes 512 | tf_op jit(solution)/shard_map/all_to_all | solution.py:36
  132.6 55.3 %all_to_all.28 = bf16[64,1,64,256]{3,2,1,0:T(8,128)(2,1)} all-to-all(bf16[64,1,64,256]{3,2,1,0:T(8,128)(2,1)S(1)} %bitcast_select_fusion.1), channel_id=1, replica_groups=mesh['wide'=64,'narrow'=4] {'wide'}, dimensions={0} | all-to-all | bytes 4194304 | tf_op jit(solution)/shard_map/all_to_all | solution.py:38
  188.5 221.1 %all-reduce.7.cloned.1.call-done = (f32[256,256]{0,1:T(8,128)}, f32[256,256]{0,1:T(8,128)}) async-done(((f32[256,256]{0,1:T(8,128)}, f32[256,256]{0,1:T(8,128)}), (f32[256,256]{0,1:T(8,128)}, f32[256,256]{0,1:T(8,128)})) %all-reduce.7.cloned.1.call-update) | async-done | bytes 524304 | tf_op jit(solution)/shard_map/psum | solution.py:79
  410.9 11.7 %cholesky.50 = f32[128,128]{1,0:T(8,128)S(1)} custom-call(f32[128,128]{1,0:T(8,128)S(1)} %cholesky.118), custom_call_target="Cholesky" | custom-call | tf_op jit(solution)/shard_map/jit(cholesky)/cholesky | solution.py:83
  422.7 9.8 %custom-call.16 = f32[1,128,128]{1,2,0:T(8,128)S(1)} custom-call(f32[1,128,128]{2,1,0:T(8,128)S(1)} %get-tuple-element.102), custom_call_target="InvertDiagBlocksLowerTriangular" | custom-call | tf_op jit(solution)/shard_map/jit(cholesky)/cholesky | solution.py:83
  433.0 11.7 %cholesky.105 = f32[128,128]{1,0:T(8,128)S(1)} custom-call(f32[128,128]{1,0:T(8,128)S(1)} %convolution_subtract_fusion), custom_call_target="Cholesky" | custom-call | tf_op jit(solution)/shard_map/jit(cholesky)/cholesky | solution.py:83
  446.7 4.0 gather_fusion.3
  450.9 4.0 gather_fusion.2
  455.1 138.6 %while.12 = (s32[]{:T(128)}, f32[4,64,256]{2,1,0:T(8,128)S(1)}, s32[24]{0:T(128)S(1)}, bf16[24,64,4096]{2,1,0:T(8,128)(2,1)}, bf16[24,64,256]{2,1,0:T(8,128)(2,1...) while((s32[]{:T(128)}, f32[4,64,256]{2,1,0:T(8,128)S(1)}, ...), condition=%wide.region_6.8_spmd, body=%wide.region_4.7_spmd.sunk | while | flops 136380432 | bytes 5179060 | solution.py:63
  464.7 2.1 fusion.48
  470.5 2.1 fusion.48
  482.0 2.1 fusion.48
  487.8 2.1 fusion.48
  505.1 2.1 fusion.48
  510.9 2.1 fusion.48
  522.4 2.1 fusion.48
  594.5 4.1 while.13
  598.5 19.7 %custom-call.17 = f32[2,128,128]{1,2,0:T(8,128)S(1)} custom-call(f32[2,128,128]{2,1,0:T(8,128)S(1)} %get-tuple-element.58), custom_call_target="InvertDiagBlocksLowerTriangular" | custom-call | tf_op jit(solution)/shard_map/triangular_solve | solution.py:84
  (201 shorter events, 109.6 us)
Async XLA Ops:
  7.4 49.9 %copy-start = (bf16[512,256]{1,0:T(8,128)(2,1)S(1)}, bf16[512,256]{1,0:T(8,128)(2,1)}, u32[]{:S(2)}) copy-start(bf16[512,256]{1,0:T(8,128)(2,1)} %param.16) | copy-start | bytes 786436
  7.4 41.0 %copy-start.1 = (bf16[128,256]{1,0:T(8,128)(2,1)S(1)}, bf16[128,256]{1,0:T(8,128)(2,1)}, u32[]{:S(2)}) copy-start(bf16[128,256]{1,0:T(8,128)(2,1)} %param.17) | copy-start | bytes 196612
  50.6 55.8 %all-to-all-start.3 = ((bf16[64,1,64,256]{3,2,1,0:T(8,128)(2,1)}), bf16[64,1,64,256]{3,2,1,0:T(8,128)(2,1)S(1)}, u32[]{:S(2)}, u32[]{:S(2)}) async-start(bf16[64,1,64,256]{3,2,1,0:T(8,128)(2,1)} %bitcast_select_fusion), calls=%async_computation.3 | async-start | bytes 4194304 | tf_op jit(solution)/shard_map/all_to_all | solution.py:48
  56.2 353.4 %all-reduce.7.cloned.1.call-start = ((), (), s32[]{:S(2)}) async-start(), calls=%async_computation.8 | async-start | bytes 1048576 | tf_op jit(solution)/shard_map/psum | solution.py:79
  58.2 388.5 %all-gather.5.cloned.1.call-start = ((), (), s32[]{:S(2)}) async-start(), calls=%async_computation.6 | async-start | bytes 10485760 | tf_op jit(solution)/shard_map/all_gather | solution.py:49
  106.4 1.3 copy-start.2
  107.7 343.1 %all-gather.3.cloned.1.call-start = ((), (), s32[]{:S(2)}) async-start(), calls=%async_computation.5 | async-start | bytes 10485760 | tf_op jit(solution)/shard_map/all_gather | solution.py:39
  187.9 0.7 copy-start.5
  187.9 430.3 %reduce-scatter.2.cloned.1.call-start = ((), (), s32[]{:S(2)}) async-start(), calls=%async_computation.7 | async-start | bytes 327680 | tf_op jit(solution)/shard_map/reduce_scatter | solution.py:68
  450.8 4.2 copy-start.4
  593.7 0.7 copy-start.3
Sparse Core Ops, SparseCore 0:
  62.7 346.9 all-reduce.6
Sparse Core Ops, SparseCore 1:
  107.8 82.2 all-gather.4
  191.8 86.7 all-gather.2
  594.5 22.1 reduce-scatter.1
where the time goes:
time: 632 us; the launch traced here: 629 us
  waiting for transfers between devices  269 us (43%)
  blocking collectives  101 us (16%)
  other arithmetic  96.6 us (15%)
  matrix products  54.9 us (9%)
  local copies, waits for them, and re-layouts  42.9 us (7%)
  loops' own time  41.5 us (7%)
  between operations  17.4 us (3%)
    psum x1, waiting for transfers between devices, body(): lax.psum((gram_share(second_factor), gram_share(third_factor)), ('wide',...  221 us
    all_to_all x1, blocking collectives, body(): lax.all_to_all(replies, 'wide', split_axis=0, concat_axis=0, tiled=True)  55.3 us
    dot_general x24, matrix products, one_block(): jnp.dot(block_data, product, preferred_element_type=jnp.float32)  49.8 us
    all_to_all x1, waiting for transfers between devices, body(): lax.all_to_all(replies, 'wide', split_axis=0, concat_axis=0, tiled=True)  48.2 us
    another operation x1, loops' own time, body(): lax.scan(one_block, jnp.zeros((R1_DEV, BS, R), jnp.float32), (tensor_bloc...  41.4 us
    all_to_all x2, blocking collectives, body(): lax.all_to_all(mine, 'wide', split_axis=0, concat_axis=0, tiled=True)  36.6 us
    another operation x6, other arithmetic, body(): cholesky_factor = jnp.linalg.cholesky(normal)  34 us
    another operation x3, other arithmetic, body(): lax.linalg.triangular_solve(cholesky_factor, partial_value, left_side=Fal...  19.7 us
  transfers between devices with their start and end apart: 5, of which 2 were waited for; matrix products, arithmetic and copies ran while one was open for 12% of the time, Pallas kernels for 0%

commit v1 on v0

v1 whole, which is shorter than its diff:
```python
import functools
import jax
import jax.numpy as jnp
from jax import lax
from jax.experimental import pallas as pl
from jax.experimental.pallas import tpu as pltpu
from jax.sharding import Mesh, PartitionSpec as P

BS = 64
R = 256
BLK = 24
YS, ZS, CS, XS = 4, 8, 2, 4
PEERS = YS * CS * XS
RING = ("y", "c", "x")
ROWS0 = 32
ROWS1 = 192
ROWS2 = 112
F32 = jnp.float32
BF16 = jnp.bfloat16
VMEM = pl.BlockSpec(memory_space=pltpu.VMEM)
SMEM = pl.BlockSpec(memory_space=pltpu.SMEM)
LIMIT = 48 * 1024 * 1024


def call(kernel, out_shape, in_specs, scratch=(), **kw):
    return pl.pallas_call(
        kernel,
        out_shape=out_shape,
        in_specs=in_specs,
        out_specs=jax.tree.map(lambda _: VMEM, out_shape),
        scratch_shapes=list(scratch),
        compiler_params=pltpu.CompilerParams(vmem_limit_bytes=LIMIT),
        **kw,
    )


def three(value):
    high = value.astype(BF16).astype(F32)
    rest = value - high
    middle = rest.astype(BF16).astype(F32)
    return high, middle, rest - middle


def halves(rows):
    return pltpu.VMEM((2, rows, 128), F32)


def put(wide, start, stride, values):
    for half in range(2):
        wide[half, pl.ds(start, PEERS, stride=stride), :] = values[:, 128 * half : 128 * half + 128]


def take(wide, start, stride):
    return jnp.concatenate([wide[half, pl.ds(start, PEERS, stride=stride), :] for half in range(2)], axis=1)


def fill(wide, values):
    for half in range(2):
        wide[half] = values[:, 128 * half : 128 * half + 128]


def whole(wide):
    return jnp.concatenate([wide[half] for half in range(2)], axis=1)


def packed_gram(rows):
    gram = lax.dot_general(rows, rows, (((0,), (0,)), ((), ())), preferred_element_type=F32)
    half = R // 2
    down = lax.broadcasted_iota(jnp.int32, (half, half), 0)
    along = lax.broadcasted_iota(jnp.int32, (half, half), 1)
    corner = gram[half:, half:]
    mixed = jnp.where(down >= along, gram[:half, :half], corner)
    diagonal = jnp.sum(jnp.where(down == along, corner, 0.0), axis=1, keepdims=True)
    return jnp.concatenate([mixed, gram[half:, :half]], axis=1), diagonal


def first_kernel(x_ref, second_ref, third_ref, seconds_ref, thirds_ref, out_ref, wide, spot):
    x = x_ref[0]
    rows_two = second_ref[pl.ds(pl.multiple_of(x * 128, 128), 128), :]
    rows_three = third_ref[pl.ds(pl.multiple_of(x * 32, 32), 32), :]
    lane = lax.broadcasted_iota(jnp.int32, (PEERS, R), 1)
    extra = [jnp.zeros((PEERS, R), F32) for _ in range(3)]
    for which, rows in enumerate((rows_two, rows_three)):
        packed, diagonal = packed_gram(rows)
        for part, values in enumerate(three(packed)):
            for m in range(4):
                put(wide, 12 * which + 4 * part + m, ROWS0, values[32 * m : 32 * m + 32, :])
        for part, values in enumerate(three(diagonal)):
            for m in range(4):
                extra[part] = jnp.where(
                    lane == 128 + 4 * which + m, values[32 * m : 32 * m + 32, :], extra[part]
                )
    pieces = rows_two.astype(F32)
    for n in range(4):
        put(wide, 24 + n, ROWS0, pieces[32 * n : 32 * n + 32, :])
    put(wide, 28, ROWS0, rows_three.astype(F32))
    seconds = seconds_ref[...]
    names = (seconds >> 4, seconds & 15, thirds_ref[...])
    for part in range(3):
        spot[...] = extra[part]
        spot[:, 0:BLK] = jnp.broadcast_to(names[part].astype(F32), (PEERS, BLK))
        put(wide, 29 + part, ROWS0, spot[...])
    out_ref[...] = whole(wide).astype(BF16).reshape(PEERS, ROWS0, R)


def second_kernel(got_ref, out_ref, wide, slab):
    fill(wide, got_ref[...].reshape(PEERS * ROWS0, R).astype(F32))
    total = got_ref[0].astype(F32)
    for source in range(1, PEERS):
        total = total + got_ref[source].astype(F32)
    for i in range(2):
        for u in range(2):
            slab[64 * i + 32 * u : 64 * i + 32 * u + 32, :] = take(wide, 24 + 2 * u + i, ROWS0)
    slab[128:160, :] = take(wide, 28, ROWS0)
    chunks = [total[12 * w : 12 * w + 4] + total[12 * w + 4 : 12 * w + 8] + total[12 * w + 8 : 12 * w + 12] for w in range(2)]
    for w in range(2):
        for part, values in enumerate(three(chunks[w])):
            slab[160 + 12 * w + 4 * part : 164 + 12 * w + 4 * part, :] = values
    slab[184:192, :] = jnp.zeros((8, R), F32)
    for part, values in enumerate(three(total[29:30] + total[30:31] + total[31:32])):
        slab[184 + part : 185 + part, :] = values
    narrow = slab[...].astype(BF16)
    for z in range(ZS):
        out_ref[z] = narrow


def third_kernel(got_ref, pick_two_ref, pick_left_ref, pick_right_ref, out_ref, wide):
    for i in range(2):
        table = got_ref[:, 64 * i : 64 * i + 64, :].reshape(64 * ZS, R)
        rows = jnp.dot(pick_two_ref[...], table, preferred_element_type=F32)
        for d in range(PEERS):
            wide[d * ROWS2 + BLK * i : d * ROWS2 + BLK * (i + 1), :] = rows[BLK * d : BLK * (d + 1)]
    table = got_ref[:, 128:160, :].reshape(32 * ZS, R)
    for i, pick_ref in enumerate((pick_left_ref, pick_right_ref)):
        rows = jnp.dot(pick_ref[...], table, preferred_element_type=F32)
        for d in range(PEERS):
            wide[d * ROWS2 + BLK * (2 + i) : d * ROWS2 + BLK * (3 + i), :] = rows[BLK * d : BLK * (d + 1)]
    total = got_ref[0, 160:192, :].astype(F32)
    for z in range(1, ZS):
        total = total + got_ref[z, 160:192, :].astype(F32)
    gram_two = total[0:4] + total[4:8] + total[8:12]
    gram_three = total[12:16] + total[16:20] + total[20:24]
    normal = three(gram_two * gram_three)
    diagonal = total[24:25] + total[25:26] + total[26:27]
    diagonal = three(diagonal[:, 128:132] * diagonal[:, 132:136])
    for part in range(3):
        wide[96 + 4 * part : 100 + 4 * part, :] = normal[part]
    wide[108:112, :] = jnp.zeros((4, R), F32)
    for part in range(3):
        wide[108 + part : 109 + part, 128:132] = diagonal[part]
    tail = wide[96:112, :]
    for d in range(1, PEERS):
        wide[d * ROWS2 + 96 : d * ROWS2 + 112, :] = tail
    out_ref[...] = wide[...].astype(BF16).reshape(PEERS, ROWS2, R)


def product_kernel(target_ref, block_ref, got_ref, out_ref, wide):
    t = pl.program_id(0)

    @pl.when(t == 0)
    def _():
        fill(wide, got_ref[...].reshape(PEERS * ROWS2, R).astype(F32))
        out_ref[...] = jnp.zeros_like(out_ref)

    left = [take(wide, BLK * i + t, ROWS2) for i in range(2)]
    right = jnp.concatenate([take(wide, BLK * (2 + i) + t, ROWS2) for i in range(2)], axis=0)
    right = right.astype(BF16)
    total = jnp.zeros((BS, R), F32)
    for q in range(BS // 4):
        parts = []
        for b in range(4 * q, 4 * q + 4):
            row = left[b // 32][b % 32 : b % 32 + 1, :]
            row = jnp.broadcast_to(row, (16, R)).astype(BF16)
            parts.append(jnp.concatenate([row] * 4, axis=0) * right)
        total = total + jnp.dot(
            block_ref[0, :, 256 * q : 256 * q + 256],
            jnp.concatenate(parts, axis=0),
            preferred_element_type=F32,
        )
    place = pl.multiple_of(target_ref[t] * BS, BS)
    out_ref[pl.ds(place, BS), :] += total


def products(targets, tensor_blocks, got):
    return pl.pallas_call(
        product_kernel,
        out_shape=jax.ShapeDtypeStruct((XS * BS, R), F32),
        grid_spec=pltpu.PrefetchScalarGridSpec(
            num_scalar_prefetch=1,
            grid=(BLK,),
            in_specs=[
                pl.BlockSpec((1, BS, BS * BS), lambda t, _: (t, 0, 0)),
                pl.BlockSpec((PEERS, ROWS2, R), lambda t, _: (0, 0, 0)),
            ],
            out_specs=pl.BlockSpec((XS * BS, R), lambda t, _: (0, 0)),
            scratch_shapes=[halves(PEERS * ROWS2)],
        ),
        compiler_params=pltpu.CompilerParams(
            vmem_limit_bytes=LIMIT, dimension_semantics=("arbitrary",)
        ),
        cost_estimate=pl.CostEstimate(
            flops=2 * BLK * BS * BS * BS * R, bytes_accessed=BLK * BS * BS * BS * 2, transcendentals=0
        ),
    )(targets, tensor_blocks, got)


def dot_high(a, b, dims=((1,), (0,))):
    return lax.dot_general(
        a, b, (dims, ((), ())), precision=lax.Precision.HIGHEST, preferred_element_type=F32
    )


def inverse_of_lower(matrix, down, along):
    size = R // 2
    joined = jnp.concatenate([matrix, jnp.where(down == along, 1.0, 0.0).astype(F32)], axis=1)
    groups = [joined[8 * g : 8 * g + 8] for g in range(size // 8)]
    sub = lax.broadcasted_iota(jnp.int32, (8, 1), 0)
    for k in range(size):
        g0, r0 = divmod(k, 8)
        pivot_row = groups[g0][r0 : r0 + 1, :]
        scaled = pivot_row * (1.0 / pivot_row[:, k : k + 1])
        for g in range(g0, size // 8):
            column = groups[g][:, k : k + 1]
            if g == g0:
                column = jnp.where(sub > r0, column, 0.0)
            groups[g] = groups[g] - column * scaled
    joined = jnp.concatenate(groups, axis=0)
    pivots = jnp.sum(jnp.where(down == along, joined[:, :size], 0.0), axis=1, keepdims=True)
    root = lax.rsqrt(pivots)
    root = root * (1.5 - 0.5 * pivots * root * root)
    return joined[:, size:] * root


def cholesky_kernel(got_ref, out_ref, wide):
    half = R // 2
    fill(wide, got_ref[...].reshape(PEERS * 16, R).astype(F32))
    packed, diagonal = [], []
    for m in range(4):
        rows = [take(wide, 4 * part + m, 16) for part in range(3)]
        packed.append(rows[0] + rows[1] + rows[2])
        rows = [take(wide, 12 + part, 16) for part in range(3)]
        diagonal.append((rows[0] + rows[1] + rows[2])[:, 128 + m : 129 + m])
    packed = jnp.concatenate(packed, axis=0)
    diagonal = jnp.concatenate(diagonal, axis=0)
    down = lax.broadcasted_iota(jnp.int32, (half, half), 0)
    along = lax.broadcasted_iota(jnp.int32, (half, half), 1)
    mixed = packed[:, :half]
    flipped = mixed.T
    upper = jnp.where(down >= along, mixed, flipped)
    corner = jnp.where(down == along, diagonal, jnp.where(down < along, mixed, flipped))
    below = packed[:, half:]
    first = inverse_of_lower(upper, down, along)
    lower = dot_high(below, first, ((1,), (1,)))
    rest = corner - dot_high(lower, lower, ((1,), (1,)))
    middle = dot_high(lower, first)
    last = inverse_of_lower(rest, down, along)
    out_ref[:half, :half] = first
    out_ref[:half, half:] = jnp.zeros((half, half), F32)
    out_ref[half:, :half] = -dot_high(last, middle)
    out_ref[half:, half:] = last


def cholesky_inverse(got):
    return pl.pallas_call(
        cholesky_kernel,
        out_shape=jax.ShapeDtypeStruct((R, R), F32),
        grid=(1,),
        in_specs=[pl.BlockSpec((PEERS, 16, R), lambda i: (0, 6, 0))],
        out_specs=pl.BlockSpec((R, R), lambda i: (0, 0)),
        scratch_shapes=[halves(PEERS * 16)],
        compiler_params=pltpu.CompilerParams(vmem_limit_bytes=LIMIT),
        cost_estimate=pl.CostEstimate(flops=10**9, bytes_accessed=10**6, transcendentals=0),
    )(got)


def final_kernel(parts_ref, inverse_ref, out_ref):
    rows = (parts_ref[0] + parts_ref[1]) + (parts_ref[2] + parts_ref[3])
    inverse = inverse_ref[...]
    halfway = dot_high(rows, inverse, ((1,), (1,)))
    out_ref[...] = dot_high(halfway, inverse)


def body(tensor_blocks, block_rows, block_seconds, block_thirds, second_factor, third_factor):
    shape = jax.ShapeDtypeStruct
    exchange = functools.partial(lax.all_to_all, split_axis=0, concat_axis=0, tiled=True)
    x = lax.axis_index("x").astype(jnp.int32).reshape(1)
    wide_at = (lax.axis_index("y") * ZS + lax.axis_index("z")) * CS + lax.axis_index("c")
    targets = block_rows - wide_at * XS

    sent = call(
        first_kernel,
        shape((PEERS, ROWS0, R), BF16),
        [SMEM, VMEM, VMEM, VMEM, VMEM],
        [halves(PEERS * ROWS0), pltpu.VMEM((PEERS, R), F32)],
    )(x, second_factor, third_factor, block_seconds.reshape(1, BLK), block_thirds.reshape(1, BLK))
    got0 = exchange(sent, RING)

    sent = call(
        second_kernel,
        shape((ZS, ROWS1, R), BF16),
        [VMEM],
        [halves(PEERS * ROWS0), pltpu.VMEM((ROWS1, R), F32)],
    )(got0)
    got1 = exchange(sent, "z")

    names = got0[:, 29:32, :BLK].astype(jnp.int32)
    seconds = (names[:, 0] * 16 + names[:, 1]).reshape(-1)
    thirds = names[:, 2].reshape(-1)

    def source(holder):
        return (holder // (ZS * CS)) * CS + holder % CS, holder // CS % ZS

    pair, plane = source(seconds // 8)
    place_two = plane * 64 + seconds % 2 * 32 + pair * XS + seconds % 8 // 2
    pair, plane = source(thirds // 2)
    place_three = plane * 32 + pair * XS + thirds % 2 * 2

    def one_hot(place, width):
        return (place[:, None] == jnp.arange(width)[None, :]).astype(BF16)

    sent = call(
        third_kernel,
        shape((PEERS, ROWS2, R), BF16),
        [VMEM] * 4,
        [pltpu.VMEM((PEERS * ROWS2, R), F32)],
    )(got1, one_hot(place_two, 64 * ZS), one_hot(place_three, 32 * ZS), one_hot(place_three + 1, 32 * ZS))
    got2 = exchange(sent, RING)

    summed = products(targets, tensor_blocks, got2)
    parts = exchange(summed.reshape(XS, BS, R), "x")
    inverse = cholesky_inverse(got2)
    return call(final_kernel, shape((BS, R), F32), [VMEM] * 2)(parts, inverse)


def solution(mesh):
    fine = Mesh(mesh.devices.reshape(YS, ZS, CS, XS), ("y", "z", "c", "x"))
    wide, every = ("y", "z", "c"), ("y", "z", "c", "x")
    in_specs = (
        P(every, None, None),
        P(every),
        P(every),
        P(every),
        P(wide, None),
        P(wide, None),
    )
    return jax.shard_map(body, mesh=fine, in_specs=in_specs, out_specs=P(every, None), check_vma=False)
```

time: 632 us -> 137 us (0.22)
  waiting for transfers between devices: 269 us -> 46.8 us
  other arithmetic: 96.6 us -> 0.67 us
  blocking collectives: 101 us -> 18 us
  matrix products: 54.9 us -> 0 us
  Pallas kernels: 0 us -> 49.4 us
  loops' own time: 41.5 us -> 0 us
  local copies, waits for them, and re-layouts: 42.9 us -> 3.26 us
  between operations: 17.4 us -> 0.11 us
  starting transfers between devices: 5.93 us -> 17.2 us
    psum x1 -> x0, waiting for transfers between devices: 221 us -> none  [body(): lax.psum((gram_share(second_factor), gram_share(third_factor)), ('wide',...]
    all_to_all x3 -> x1, blocking collectives: 91.8 us -> 18 us  [body(): got0 = exchange(sent, RING)]
    another operation x34 -> x0, other arithmetic: 71.2 us -> none  [the longest x6 34 us: body(): cholesky_factor = jnp.linalg.cholesky(normal)]
    dot_general x26 -> x0, matrix products: 51.6 us -> none  [the longest x24 49.8 us: one_block(): jnp.dot(block_data, product, preferred_element_type=jnp.float32)]
    pallas_call x0 -> x6, Pallas kernels: none -> 49.4 us  [the longest x1 22.6 us: cholesky_inverse(): pl.pallas_call(cholesky_kernel, out_shape=jax.ShapeDtypeStruct((R, R), F3...]
    another operation x2 -> x0, loops' own time: 41.5 us -> none  [the longest x1 41.4 us: body(): lax.scan(one_block, jnp.zeros((R1_DEV, BS, R), jnp.float32), (tensor_bloc...]
    convert_element_type x24 -> x3, other arithmetic: 16.4 us -> 0.5 us  [the longest x2 0.46 us: one_hot(): return (place[:, None] == jnp.arange(width)[None, :]).astype(BF16)]
    dynamic_slice x24 -> x0, local copies, waits for them, and re-layouts: 13.9 us -> none  [body(): lax.scan(one_block, jnp.zeros((R1_DEV, BS, R), jnp.float32), (tensor_bloc...]
  transfers between devices with their start and end apart: 5 -> 3, of which waited for: 2 -> 2; matrix products, arithmetic and copies ran while one was open for 12% -> 1% of each run, Pallas kernels for 0% -> 17%
where the time goes in v1:
time: 137 us; the launch traced here: 135 us
  Pallas kernels  49.4 us (36%)
  waiting for transfers between devices  46.8 us (34%)
  blocking collectives  18 us (13%)
  starting transfers between devices  17.2 us (13%)
  local copies, waits for them, and re-layouts  3.26 us (2%)
    all_to_all x1, waiting for transfers between devices, body(): got2 = exchange(sent, RING)  24.5 us
    pallas_call x1, Pallas kernels, cholesky_inverse(): pl.pallas_call(cholesky_kernel, out_shape=jax.ShapeDtypeStruct((R, R), F3...  22.6 us
    all_to_all x1, waiting for transfers between devices, body(): got1 = exchange(sent, 'z')  22.3 us
    pallas_call x1, Pallas kernels, products(): pl.pallas_call(product_kernel, out_shape=jax.ShapeDtypeStruct((XS * BS, R...  21.1 us
    all_to_all x1, blocking collectives, body(): got0 = exchange(sent, RING)  18 us
    all_to_all x1, starting transfers between devices, body(): got1 = exchange(sent, 'z')  8.46 us
    all_to_all x1, starting transfers between devices, body(): got2 = exchange(sent, RING)  5.19 us
    all_to_all x1, starting transfers between devices, body(): parts = exchange(summed.reshape(XS, BS, R), 'x')  3.58 us
  transfers between devices with their start and end apart: 3, of which 2 were waited for; matrix products, arithmetic and copies ran while one was open for 1% of the time, Pallas kernels for 17%

profile of v1, /device:TPU:8, one launch (start us, length us, event | category | flops | bytes accessed | tf_op | source)
XLA Modules:
  0.0 135.4 jit_solution(17152163111530765787)
XLA Ops:
  0.0 0.0 copy-start
  0.0 0.9 copy-done
  1.0 0.8 copy-done.1
  1.8 0.7 copy-done.2
  2.4 0.7 copy-done.3
  3.1 1.1 shard_map.64
  4.2 18.0 %all_to_all.20.got_ref = bf16[32,32,256]{2,1,0:T(8,128)(2,1)S(1)} all-to-all(bf16[32,32,256]{2,1,0:T(8,128)(2,1)S(1)} %shard_map.64), channel_id=1, replica_groups=mesh['y'=4,'z'=8,'c'=2,'x'=4] {'y','c','x'}, dimensions={0} | all-to-all | bytes 1048576 | tf_op jit(solution)/shard_map/all_to_all | solution.py:296
  22.2 1.1 shard_map.65
  23.3 8.5 %all-to-all-start.1 = ((bf16[8,192,256]{2,1,0:T(8,128)(2,1)}), bf16[8,192,256]{2,1,0:T(8,128)(2,1)S(1)}, u32[]{:S(2)}, u32[]{:S(2)}) async-start(bf16[8,192,256]{2,1,0:T(8,128)(2,1)} %shard_map.65), calls=%async_computation.1 | async-start | bytes 1572864 | tf_op jit(solution)/shard_map/all_to_all | solution.py:304
  31.8 0.1 slice_reduce_fusion
  32.0 0.1 reshape_squeeze.3
  32.0 0.1 add.197
  32.2 0.2 fusion.pick_two_ref
  32.4 0.3 fusion.1
  32.7 22.3 %all-to-all-done.1.got_ref = bf16[8,192,256]{2,1,0:T(8,128)(2,1)S(1)} async-done(((bf16[8,192,256]{2,1,0:T(8,128)(2,1)}), bf16[8,192,256]{2,1,0:T(8,128)(2,1)S(1)}, u32[]{:S(2)}, u32[]{:S(2)}) %all-to-all-start.1) | async-done | bytes 786464 | tf_op jit(solution)/shard_map/all_to_all | solution.py:304
  55.0 2.0 %shard_map.66 = bf16[32,112,256]{2,1,0:T(8,128)(2,1)} custom-call(bf16[8,192,256]{2,1,0:T(8,128)(2,1)S(1)} %all-to-all-done.1.got_ref, bf16[768,512]{1,0:T(8,128)(2,1)S(1)} %fusion.pick_two_ref, bf16[768,256]{1,0:T(8,128)(2,1)S(1)} %get-tuple-element.9.pick_left_ref, bf16[768,256]{1,0:T(8,128)(2,1)S(1)} %get-tuple-element.10.pick_right_ref), custom_call_target="tpu_custom_call" | custom-call | tf_op jit(solution)/shard_map/pallas_call | solution.py:321
  57.0 5.2 %all-to-all-start.2 = ((bf16[32,112,256]{2,1,0:T(8,128)(2,1)}), bf16[32,112,256]{2,1,0:T(8,128)(2,1)S(1)}, u32[]{:S(2)}, u32[]{:S(2)}) async-start(bf16[32,112,256]{2,1,0:T(8,128)(2,1)} %shard_map.66), calls=%async_computation.2 | async-start | bytes 3670016 | tf_op jit(solution)/shard_map/all_to_all | solution.py:327
  62.2 0.0 copy-done.4
  62.2 24.5 %all-to-all-done.2.got_ref = bf16[32,112,256]{2,1,0:T(8,128)(2,1)S(1)} async-done(((bf16[32,112,256]{2,1,0:T(8,128)(2,1)}), bf16[32,112,256]{2,1,0:T(8,128)(2,1)S(1)}, u32[]{:S(2)}, u32[]{:S(2)}) %all-to-all-start.2) | async-done | bytes 1835040 | tf_op jit(solution)/shard_map/all_to_all | solution.py:327
  86.7 21.1 %shard_map.67 = f32[256,256]{1,0:T(8,128)} custom-call(s32[24]{0:T(128)S(1)} %broadcast_subtract_fusion.target_ref, bf16[24,64,4096]{2,1,0:T(8,128)(2,1)} %block_ref.1, bf16[32,112,256]{2,1,0:T(8,128)(2,1)S(1)} %all-to-all-done.2.got_ref), custom_call_target="tpu_custom_call" | custom-call | flops 3221225472 | bytes 12582912 | tf_op jit(solution)/shard_map/pallas_call | solution.py:185
  107.8 3.6 %all-to-all-start.3 = ((f32[4,64,256]{2,1,0:T(8,128)}), f32[4,64,256]{2,1,0:T(8,128)S(1)}, u32[]{:S(2)}, u32[]{:S(2)}) async-start(f32[4,64,256]{2,1,0:T(8,128)} %bitcast.3), calls=%async_computation.3 | async-start | bytes 524288 | tf_op jit(solution)/shard_map/all_to_all | solution.py:330
  111.4 22.6 %shard_map.68.inverse_ref = f32[256,256]{1,0:T(8,128)S(1)} custom-call(bf16[32,112,256]{2,1,0:T(8,128)(2,1)S(1)} %all-to-all-done.2.got_ref), custom_call_target="tpu_custom_call" | custom-call | flops 1000000000 | bytes 1000000 | tf_op jit(solution)/shard_map/pallas_call | solution.py:264
  134.0 0.0 all-to-all-done.3.parts_ref
  134.0 1.4 %shard_map.69 = f32[64,256]{1,0:T(8,128)} custom-call(f32[4,64,256]{2,1,0:T(8,128)S(1)} %all-to-all-done.3.parts_ref, f32[256,256]{1,0:T(8,128)S(1)} %shard_map.68.inverse_ref), custom_call_target="tpu_custom_call" | custom-call | tf_op jit(solution)/shard_map/pallas_call | solution.py:332
  (8 shorter events, 0.1 us)
Async XLA Ops:
  0.0 0.9 copy-start
  1.0 0.8 copy-start.1
  1.8 0.7 copy-start.2
  2.4 0.7 copy-start.3
  23.3 31.6 %all-to-all-start.1 = ((bf16[8,192,256]{2,1,0:T(8,128)(2,1)}), bf16[8,192,256]{2,1,0:T(8,128)(2,1)S(1)}, u32[]{:S(2)}, u32[]{:S(2)}) async-start(bf16[8,192,256]{2,1,0:T(8,128)(2,1)} %shard_map.65), calls=%async_computation.1 | async-start | bytes 1572864 | tf_op jit(solution)/shard_map/all_to_all | solution.py:304
  57.0 5.2 %copy-start.4 = (s32[24]{0:T(128)S(1)}, s32[24]{0:T(128)}, u32[]{:S(2)}) copy-start(s32[24]{0:T(128)} %param.7) | copy-start | bytes 292
  57.0 29.7 %all-to-all-start.2 = ((bf16[32,112,256]{2,1,0:T(8,128)(2,1)}), bf16[32,112,256]{2,1,0:T(8,128)(2,1)S(1)}, u32[]{:S(2)}, u32[]{:S(2)}) async-start(bf16[32,112,256]{2,1,0:T(8,128)(2,1)} %shard_map.66), calls=%async_computation.2 | async-start | bytes 3670016 | tf_op jit(solution)/shard_map/all_to_all | solution.py:327
  107.8 26.2 %all-to-all-start.3 = ((f32[4,64,256]{2,1,0:T(8,128)}), f32[4,64,256]{2,1,0:T(8,128)S(1)}, u32[]{:S(2)}, u32[]{:S(2)}) async-start(f32[4,64,256]{2,1,0:T(8,128)} %bitcast.3), calls=%async_computation.3 | async-start | bytes 524288 | tf_op jit(solution)/shard_map/all_to_all | solution.py:330

commit v2 on v1

v2 whole, which is shorter than its diff:
```python
import functools
import jax
import jax.numpy as jnp
from jax import lax
from jax.experimental import pallas as pl
from jax.experimental.pallas import tpu as pltpu
from jax.sharding import Mesh, PartitionSpec as P

BS = 64
R = 256
BLK = 24
YS, ZS, CS, XS = 4, 8, 2, 4
PEERS = YS * CS * XS
RING = ("y", "c", "x")
ROWS0 = 32
ROWS1 = 192
ROWS2 = 112
F32 = jnp.float32
BF16 = jnp.bfloat16
VMEM = pl.BlockSpec(memory_space=pltpu.VMEM)
SMEM = pl.BlockSpec(memory_space=pltpu.SMEM)
HBM = pl.BlockSpec(memory_space=pltpu.HBM)
LIMIT = 48 * 1024 * 1024


def call(kernel, out_shape, in_specs, scratch=(), **kw):
    return pl.pallas_call(
        kernel,
        out_shape=out_shape,
        in_specs=in_specs,
        out_specs=jax.tree.map(lambda _: VMEM, out_shape),
        scratch_shapes=list(scratch),
        compiler_params=pltpu.CompilerParams(vmem_limit_bytes=LIMIT),
        **kw,
    )


def three(value):
    high = value.astype(BF16).astype(F32)
    rest = value - high
    middle = rest.astype(BF16).astype(F32)
    return high, middle, rest - middle


def halves(rows):
    return pltpu.VMEM((2, rows, 128), F32)


def put(wide, start, stride, values):
    for half in range(2):
        wide[half, pl.ds(start, PEERS, stride=stride), :] = values[:, 128 * half : 128 * half + 128]


def take(wide, start, stride):
    return jnp.concatenate([wide[half, pl.ds(start, PEERS, stride=stride), :] for half in range(2)], axis=1)


def fill(wide, values):
    for half in range(2):
        wide[half] = values[:, 128 * half : 128 * half + 128]


def whole(wide):
    return jnp.concatenate([wide[half] for half in range(2)], axis=1)


def packed_gram(rows):
    gram = lax.dot_general(rows, rows, (((0,), (0,)), ((), ())), preferred_element_type=F32)
    half = R // 2
    down = lax.broadcasted_iota(jnp.int32, (half, half), 0)
    along = lax.broadcasted_iota(jnp.int32, (half, half), 1)
    corner = gram[half:, half:]
    mixed = jnp.where(down >= along, gram[:half, :half], corner)
    diagonal = jnp.sum(jnp.where(down == along, corner, 0.0), axis=1, keepdims=True)
    return jnp.concatenate([mixed, gram[half:, :half]], axis=1), diagonal


def first_kernel(x_ref, second_ref, third_ref, seconds_ref, thirds_ref, out_ref, wide, spot, two, few, at, sems):
    x = x_ref[0]
    copies = [
        pltpu.make_async_copy(second_ref.at[pl.ds(pl.multiple_of(x * 128, 128), 128), :], two, sems.at[0]),
        pltpu.make_async_copy(third_ref.at[pl.ds(pl.multiple_of(x * 32, 32), 32), :], few, sems.at[1]),
        pltpu.make_async_copy(seconds_ref, at.at[0], sems.at[2]),
        pltpu.make_async_copy(thirds_ref, at.at[1], sems.at[3]),
    ]
    for copy in copies:
        copy.start()
    for copy in copies:
        copy.wait()
    rows_two = two[...]
    rows_three = few[...]
    lane = lax.broadcasted_iota(jnp.int32, (PEERS, R), 1)
    extra = [jnp.zeros((PEERS, R), F32) for _ in range(3)]
    for which, rows in enumerate((rows_two, rows_three)):
        packed, diagonal = packed_gram(rows)
        for part, values in enumerate(three(packed)):
            for m in range(4):
                put(wide, 12 * which + 4 * part + m, ROWS0, values[32 * m : 32 * m + 32, :])
        for part, values in enumerate(three(diagonal)):
            for m in range(4):
                extra[part] = jnp.where(
                    lane == 128 + 4 * which + m, values[32 * m : 32 * m + 32, :], extra[part]
                )
    pieces = rows_two.astype(F32)
    for n in range(4):
        put(wide, 24 + n, ROWS0, pieces[32 * n : 32 * n + 32, :])
    put(wide, 28, ROWS0, rows_three.astype(F32))
    seconds = at[0]
    names = (seconds >> 4, seconds & 15, at[1])
    for part in range(3):
        spot[...] = extra[part]
        spot[:, 0:BLK] = jnp.broadcast_to(names[part].astype(F32), (PEERS, BLK))
        put(wide, 29 + part, ROWS0, spot[...])
    out_ref[...] = whole(wide).astype(BF16).reshape(PEERS, ROWS0, R)


def second_kernel(got_ref, out_ref, wide, slab):
    fill(wide, got_ref[...].reshape(PEERS * ROWS0, R).astype(F32))
    total = got_ref[0].astype(F32)
    for source in range(1, PEERS):
        total = total + got_ref[source].astype(F32)
    for i in range(2):
        for u in range(2):
            slab[64 * i + 32 * u : 64 * i + 32 * u + 32, :] = take(wide, 24 + 2 * u + i, ROWS0)
    slab[128:160, :] = take(wide, 28, ROWS0)
    chunks = [total[12 * w : 12 * w + 4] + total[12 * w + 4 : 12 * w + 8] + total[12 * w + 8 : 12 * w + 12] for w in range(2)]
    for w in range(2):
        for part, values in enumerate(three(chunks[w])):
            slab[160 + 12 * w + 4 * part : 164 + 12 * w + 4 * part, :] = values
    slab[184:192, :] = jnp.zeros((8, R), F32)
    for part, values in enumerate(three(total[29:30] + total[30:31] + total[31:32])):
        slab[184 + part : 185 + part, :] = values
    out_ref[...] = slab[...].astype(BF16)


def third_kernel(*refs):
    pieces = refs[:ZS]
    pick_two_ref, pick_left_ref, pick_right_ref, out_ref, wide = refs[ZS:]

    def table(start, stop):
        return jnp.concatenate([ref[start:stop, :] for ref in pieces], axis=0)

    for i in range(2):
        rows = jnp.dot(pick_two_ref[...], table(64 * i, 64 * i + 64), preferred_element_type=F32)
        for d in range(PEERS):
            wide[d * ROWS2 + BLK * i : d * ROWS2 + BLK * (i + 1), :] = rows[BLK * d : BLK * (d + 1)]
    for i, pick_ref in enumerate((pick_left_ref, pick_right_ref)):
        rows = jnp.dot(pick_ref[...], table(128, 160), preferred_element_type=F32)
        for d in range(PEERS):
            wide[d * ROWS2 + BLK * (2 + i) : d * ROWS2 + BLK * (3 + i), :] = rows[BLK * d : BLK * (d + 1)]
    total = pieces[0][160:, :].astype(F32)
    for ref in pieces[1:]:
        total = total + ref[160:, :].astype(F32)
    gram_two = total[0:4] + total[4:8] + total[8:12]
    gram_three = total[12:16] + total[16:20] + total[20:24]
    normal = three(gram_two * gram_three)
    diagonal = total[24:25] + total[25:26] + total[26:27]
    diagonal = three(diagonal[:, 128:132] * diagonal[:, 132:136])
    for part in range(3):
        wide[96 + 4 * part : 100 + 4 * part, :] = normal[part]
    wide[108:112, :] = jnp.zeros((4, R), F32)
    for part in range(3):
        wide[108 + part : 109 + part, 128:132] = diagonal[part]
    tail = wide[96:112, :]
    for d in range(1, PEERS):
        wide[d * ROWS2 + 96 : d * ROWS2 + 112, :] = tail
    out_ref[...] = wide[...].astype(BF16).reshape(PEERS, ROWS2, R)


def dot_high(a, b, dims=((1,), (0,))):
    return lax.dot_general(
        a, b, (dims, ((), ())), precision=lax.Precision.HIGHEST, preferred_element_type=F32
    )


def reciprocal(value):
    guess = pltpu.reciprocal(value, approx=True)
    return guess * (2.0 - value * guess)


def inverse_root(value):
    guess = lax.rsqrt(value)
    return guess * (1.5 - 0.5 * value * guess * guess)


def eliminate(matrix, down, along):
    size = R // 2
    count = size // 8
    identity = jnp.where(down == along, 1.0, 0.0).astype(F32)
    left = [matrix[8 * g : 8 * g + 8] for g in range(count)]
    right = [identity[8 * g : 8 * g + 8] for g in range(count)]
    sub = lax.broadcasted_iota(jnp.int32, (8, size), 0)

    def row(value, j):
        return jnp.broadcast_to(value[j : j + 1, :], (8, size))

    def columns(g, p):
        return [jnp.broadcast_to(left[g][:, 8 * p + j : 8 * p + j + 1], (8, size)) for j in range(8)]

    for p in range(count):
        pivots = []
        for g in range(p, count):
            spread = columns(g, p)
            new_left, new_right = left[g], right[g]
            for n in range(4):
                j = 2 * n
                if g == p:
                    across = [[row(spread[m], j + i) for m in range(8)] for i in range(2)]
                    a, b, d = across[0][j], across[0][j + 1], across[1][j + 1]
                    scale = reciprocal(a * d - b * b)
                    rows = [row(new_left, j), row(new_left, j + 1), row(new_right, j), row(new_right, j + 1)]
                    pivots.append((across, a, b, d, scale, rows))
                    if n == 3:
                        break
                    first = jnp.where(sub > j + 1, spread[j], 0.0)
                    second = jnp.where(sub > j + 1, spread[j + 1], 0.0)
                else:
                    across, a, b, d, scale, rows = pivots[n]
                    first, second = spread[j], spread[j + 1]
                one = (first * d - second * b) * scale
                two = (second * a - first * b) * scale
                for m in range(j + 2, 8):
                    spread[m] = spread[m] - (one * across[0][m] + two * across[1][m])
                new_left = new_left - (one * rows[0] + two * rows[1])
                new_right = new_right - (one * rows[2] + two * rows[3])
            left[g], right[g] = new_left, new_right
        yield
    left = jnp.concatenate(left, axis=0)
    right = jnp.concatenate(right, axis=0)
    main = jnp.sum(jnp.where(down == along, left, 0.0), axis=1, keepdims=True)
    below = jnp.sum(jnp.where(down == along + 1, left, 0.0), axis=1, keepdims=True)
    above = pltpu.roll(jnp.broadcast_to(main, (size, size)), 1, 0)[:, :1]
    odd = lax.broadcasted_iota(jnp.int32, (size, 1), 0) % 2 == 1
    ratio = jnp.where(odd, below / above, 0.0)
    return (right - ratio * pltpu.roll(right, 1, 0)) * inverse_root(main - ratio * below)


def finish(steps):
    while True:
        try:
            next(steps)
        except StopIteration as stop:
            return stop.value


def scaled_normal(wide, down, along):
    half = R // 2
    packed, diagonal = [], []
    for m in range(4):
        rows = [take(wide, 96 + 4 * part + m, ROWS2) for part in range(3)]
        packed.append(rows[0] + rows[1] + rows[2])
        rows = [take(wide, 108 + part, ROWS2) for part in range(3)]
        diagonal.append((rows[0] + rows[1] + rows[2])[:, 128 + m : 129 + m])
    packed = jnp.concatenate(packed, axis=0)
    diagonal = jnp.concatenate(diagonal, axis=0)
    mixed = packed[:, :half]
    flipped = mixed.T
    upper = jnp.where(down >= along, mixed, flipped)
    corner = jnp.where(down == along, diagonal, jnp.where(down < along, mixed, flipped))
    scales = [
        [inverse_root(jnp.sum(jnp.where(down == along, part, 0.0), axis=axis, keepdims=True)) for axis in (1, 0)]
        for part in (upper, corner)
    ]
    upper = upper * scales[0][0] * scales[0][1]
    below = packed[:, half:] * scales[1][0] * scales[0][1]
    corner = corner * scales[1][0] * scales[1][1]
    return upper, below, corner, scales[0][1], scales[1][1]


def product_kernel(rows_ref, base_ref, tensor_ref, got_ref, out_ref, state_ref, wide, blocks, sems):
    def fetch(t):
        return pltpu.make_async_copy(tensor_ref.at[t], blocks.at[t], sems.at[t])

    for t in range(BLK):
        fetch(t).start()
    fill(wide, got_ref[...].reshape(PEERS * ROWS2, R).astype(F32))
    out_ref[...] = jnp.zeros_like(out_ref)
    half = R // 2
    down = lax.broadcasted_iota(jnp.int32, (half, half), 0)
    along = lax.broadcasted_iota(jnp.int32, (half, half), 1)
    upper, below, corner, scale, scale_last = scaled_normal(wide, down, along)
    steps = eliminate(upper, down, along)

    def one_block(t):
        left = [take(wide, BLK * i + t, ROWS2) for i in range(2)]
        right = jnp.concatenate([take(wide, BLK * (2 + i) + t, ROWS2) for i in range(2)], axis=0)
        right = right.astype(BF16)

        total = jnp.zeros((BS, R), F32)
        for q in range(BS // 4):
            parts = []
            for b in range(4 * q, 4 * q + 4):
                row = left[b // 32][b % 32 : b % 32 + 1, :]
                row = jnp.broadcast_to(row, (16, R)).astype(BF16)
                parts.append(jnp.concatenate([row] * 4, axis=0) * right)
            total = total + jnp.dot(
                blocks[t, :, 256 * q : 256 * q + 256],
                jnp.concatenate(parts, axis=0),
                preferred_element_type=F32,
            )
        place = pl.multiple_of((rows_ref[t] - base_ref[0]) * BS, BS)
        out_ref[pl.ds(place, BS), :] += total

    taken = 0
    for t in range(BLK):
        if t % 4 == 0:
            for later in range(t, t + 4):
                fetch(later).wait()
        one_block(t)
        while taken < min(half // 8, (t + 1) * half // 8 // (BLK - 4)):
            next(steps)
            taken += 1
    first = finish(steps)
    lower = dot_high(below, first, ((1,), (1,)))
    state_ref[0] = first
    state_ref[1] = corner - dot_high(lower, lower, ((1,), (1,)))
    state_ref[2] = dot_high(lower, first)
    state_ref[3] = jnp.broadcast_to(scale, (half, half))
    state_ref[4] = jnp.broadcast_to(scale_last, (half, half))


def products(block_rows, base, tensor_blocks, got):
    return call(
        product_kernel,
        (
            jax.ShapeDtypeStruct((XS * BS, R), F32),
            jax.ShapeDtypeStruct((5, R // 2, R // 2), F32),
        ),
        [SMEM, SMEM, HBM, VMEM],
        [
            halves(PEERS * ROWS2),
            pltpu.VMEM((BLK, BS, BS * BS), BF16),
            pltpu.SemaphoreType.DMA((BLK,)),
        ],
        cost_estimate=pl.CostEstimate(
            flops=2 * BLK * BS * BS * BS * R, bytes_accessed=BLK * BS * BS * BS * 2, transcendentals=0
        ),
    )(block_rows, base, tensor_blocks, got)


def inverse_kernel(state_ref, out_ref):
    half = R // 2
    down = lax.broadcasted_iota(jnp.int32, (half, half), 0)
    along = lax.broadcasted_iota(jnp.int32, (half, half), 1)
    scale, scale_last = state_ref[3, :1], state_ref[4, :1]
    last = finish(eliminate(state_ref[1], down, along))
    out_ref[:half, :half] = state_ref[0] * scale
    out_ref[:half, half:] = jnp.zeros((half, half), F32)
    out_ref[half:, :half] = -dot_high(last, state_ref[2]) * scale
    out_ref[half:, half:] = last * scale_last


def final_kernel(parts_ref, inverse_ref, out_ref):
    rows = (parts_ref[0] + parts_ref[1]) + (parts_ref[2] + parts_ref[3])
    inverse = inverse_ref[...]
    halfway = dot_high(rows, inverse, ((1,), (1,)))
    out_ref[...] = dot_high(halfway, inverse)


def body(tensor_blocks, block_rows, block_seconds, block_thirds, second_factor, third_factor):
    shape = jax.ShapeDtypeStruct
    exchange = functools.partial(lax.all_to_all, split_axis=0, concat_axis=0, tiled=True)
    x = lax.axis_index("x").astype(jnp.int32).reshape(1)
    wide_at = (lax.axis_index("y") * ZS + lax.axis_index("z")) * CS + lax.axis_index("c")
    base = (wide_at * XS).astype(jnp.int32).reshape(1)

    keep = functools.partial(pltpu.with_memory_space_constraint, memory_space=pltpu.HBM)
    sent = call(
        first_kernel,
        shape((PEERS, ROWS0, R), BF16),
        [SMEM, HBM, HBM, HBM, HBM],
        [
            halves(PEERS * ROWS0),
            pltpu.VMEM((PEERS, R), F32),
            pltpu.VMEM((128, R), BF16),
            pltpu.VMEM((32, R), BF16),
            pltpu.VMEM((2, 1, BLK), jnp.int32),
            pltpu.SemaphoreType.DMA((4,)),
        ],
    )(x, *map(keep, (second_factor, third_factor, block_seconds.reshape(1, BLK), block_thirds.reshape(1, BLK))))
    got0 = exchange(sent, RING)

    sent = call(
        second_kernel,
        shape((ROWS1, R), BF16),
        [VMEM],
        [halves(PEERS * ROWS0), pltpu.VMEM((ROWS1, R), F32)],
    )(got0)
    around = [[(z, (z + step) % ZS) for z in range(ZS)] for step in (1, -1)]
    from_low, from_high = [sent], [sent]
    for _ in range(3):
        from_low.append(lax.ppermute(from_low[-1], "z", around[0]))
        from_high.append(lax.ppermute(from_high[-1], "z", around[1]))
    pieces = from_low + from_high[1:] + [lax.ppermute(from_low[-1], "z", around[0])]

    names = got0[:, 29:32, :BLK].astype(jnp.int32)
    seconds = (names[:, 0] * 16 + names[:, 1]).reshape(-1)
    thirds = names[:, 2].reshape(-1)

    def source(holder):
        back = (lax.axis_index("z") - holder // CS) % ZS
        return (holder // (ZS * CS)) * CS + holder % CS, jnp.where(back < 4, back, 11 - back)

    pair, plane = source(seconds // 8)
    place_two = plane * 64 + seconds % 2 * 32 + pair * XS + seconds % 8 // 2
    pair, plane = source(thirds // 2)
    place_three = plane * 32 + pair * XS + thirds % 2 * 2

    def one_hot(place, width):
        return (place[:, None] == jnp.arange(width)[None, :]).astype(BF16)

    sent = call(
        third_kernel,
        shape((PEERS, ROWS2, R), BF16),
        [VMEM] * (ZS + 3),
        [pltpu.VMEM((PEERS * ROWS2, R), F32)],
    )(*pieces, one_hot(place_two, 64 * ZS), one_hot(place_three, 32 * ZS), one_hot(place_three + 1, 32 * ZS))
    got2 = exchange(sent, RING)

    summed, state = products(block_rows, base, tensor_blocks, got2)
    parts = exchange(summed.reshape(XS, BS, R), "x")
    inverse = call(
        inverse_kernel,
        shape((R, R), F32),
        [VMEM],
        cost_estimate=pl.CostEstimate(flops=10**9, bytes_accessed=10**6, transcendentals=0),
    )(state)
    return call(final_kernel, shape((BS, R), F32), [VMEM] * 2)(parts, inverse)


def solution(mesh):
    fine = Mesh(mesh.devices.reshape(YS, ZS, CS, XS), ("y", "z", "c", "x"))
    wide, every = ("y", "z", "c"), ("y", "z", "c", "x")
    in_specs = (
        P(every, None, None),
        P(every),
        P(every),
        P(every),
        P(wide, None),
        P(wide, None),
    )
    return jax.shard_map(body, mesh=fine, in_specs=in_specs, out_specs=P(every, None), check_vma=False)
```

time: 137 us -> 109 us (0.80)
  Pallas kernels: 49.4 us -> 23.6 us
  blocking collectives: 18 us -> 0 us
  starting transfers between devices: 17.2 us -> 30 us
  waiting for transfers between devices: 46.8 us -> 52.6 us
  local copies, waits for them, and re-layouts: 3.26 us -> 1.42 us
    pallas_call x5, Pallas kernels: 48 us -> 22.2 us  [the longest x1 14 us: products(): call(product_kernel, (jax.ShapeDtypeStruct((XS * BS, R), F32), jax.ShapeD...]
    all_to_all x1 -> x0, blocking collectives: 18 us -> none  [body(): got0 = exchange(sent, RING)]
    ppermute x0 -> x7, waiting for transfers between devices: none -> 15.5 us  [the longest x3 9.86 us: body(): from_low.append(lax.ppermute(from_low[-1], 'z', around[0]))]
    ppermute x0 -> x7, starting transfers between devices: none -> 12.9 us  [the longest x3 12.9 us: body(): from_high.append(lax.ppermute(from_high[-1], 'z', around[1]))]
    all_to_all x1, waiting for transfers between devices: 22.3 us -> 10.6 us  [body(): got0 = exchange(sent, RING)]
    all_to_all x1, waiting for transfers between devices: 0.01 us -> 2.07 us  [body(): parts = exchange(summed.reshape(XS, BS, R), 'x')]
    unnamed x10 -> x4, local copies, waits for them, and re-layouts: 3.1 us -> 1.26 us
  transfers between devices with their start and end apart: 3 -> 10, of which waited for: 2 -> 7; matrix products, arithmetic and copies ran while one was open for 1% -> 1% of each run, Pallas kernels for 17% -> 4%
where the time goes in v2:
time: 109 us; the launch traced here: 108 us
  waiting for transfers between devices  52.6 us (48%)
  starting transfers between devices  30 us (28%)
  Pallas kernels  23.6 us (22%)
  local copies, waits for them, and re-layouts  1.42 us (1%)
    all_to_all x1, waiting for transfers between devices, body(): got2 = exchange(sent, RING)  24.4 us
    pallas_call x1, Pallas kernels, products(): call(product_kernel, (jax.ShapeDtypeStruct((XS * BS, R), F32), jax.ShapeD...  14 us
    ppermute x3, starting transfers between devices, body(): from_high.append(lax.ppermute(from_high[-1], 'z', around[1]))  12.9 us
    all_to_all x1, waiting for transfers between devices, body(): got0 = exchange(sent, RING)  10.6 us
    ppermute x3, waiting for transfers between devices, body(): from_low.append(lax.ppermute(from_low[-1], 'z', around[0]))  9.86 us
    all_to_all x1, starting transfers between devices, body(): got0 = exchange(sent, RING)  7.55 us
    all_to_all x1, starting transfers between devices, body(): got2 = exchange(sent, RING)  5.97 us
    ppermute x1, waiting for transfers between devices, body(): lax.ppermute(from_low[-1], 'z', around[0])  5.61 us
  transfers between devices with their start and end apart: 10, of which 7 were waited for; matrix products, arithmetic and copies ran while one was open for 1% of the time, Pallas kernels for 4%

profile of v2, /device:TPU:8, one launch (start us, length us, event | category | flops | bytes accessed | tf_op | source)
XLA Modules:
  0.0 108.5 jit_solution(3756747133010714591)
XLA Ops:
  0.0 2.8 %shard_map.64 = bf16[32,32,256]{2,1,0:T(8,128)(2,1)} custom-call(s32[1]{0:T(128)} %bitcast.1.x_ref, bf16[512,256]{1,0:T(8,128)(2,1)} %second_ref.1, bf16[128,256]{1,0:T(8,128)(2,1)} %third_ref.1, s32[1,24]{1,0:T(1,128)} %bitcast.5, s32[1,24]{1,0:T(1,128)} %bitcast.6), custom_call_target="tpu_custom_call" | custom-call | tf_op jit(solution)/shard_map/pallas_call | solution.py:368
  2.8 7.5 %all-to-all-start = ((bf16[32,32,256]{2,1,0:T(8,128)(2,1)}), bf16[32,32,256]{2,1,0:T(8,128)(2,1)S(1)}, u32[]{:S(2)}, u32[]{:S(2)}) async-start(bf16[32,32,256]{2,1,0:T(8,128)(2,1)} %shard_map.64), calls=%async_computation | async-start | bytes 1048576 | tf_op jit(solution)/shard_map/all_to_all | solution.py:381
  10.4 10.6 %all-to-all-done.got_ref = bf16[32,32,256]{2,1,0:T(8,128)(2,1)S(1)} async-done(((bf16[32,32,256]{2,1,0:T(8,128)(2,1)}), bf16[32,32,256]{2,1,0:T(8,128)(2,1)S(1)}, u32[]{:S(2)}, u32[]{:S(2)}) %all-to-all-start) | async-done | bytes 524320 | tf_op jit(solution)/shard_map/all_to_all | solution.py:381
  21.0 0.2 shard_map.65.refs_0_
  21.2 5.9 %collective-permute-start.3 = (bf16[192,256]{1,0:T(8,128)(2,1)S(1)}, bf16[192,256]{1,0:T(8,128)(2,1)S(1)}, u32[]{:S(2)}, u32[]{:S(2)}) collective-permute-start(bf16[192,256]{1,0:T(8,128)(2,1)S(1)} %shard_map.65.refs_0_), channel_id=1, source_target_pairs={{0,56},{8,0},{16,8},{24,16},{32,24},{40,32},{48,40},{56,48},{1,57}... | collective-permute-start | bytes 294920 | tf_op jit(solution)/shard_map/ppermute | solution.py:393
  27.2 0.1 slice_reduce_fusion
  27.3 0.1 reshape_squeeze.3
  27.4 5.6 %collective-permute-done.refs_1_ = bf16[192,256]{1,0:T(8,128)(2,1)S(1)} collective-permute-done((bf16[192,256]{1,0:T(8,128)(2,1)S(1)}, bf16[192,256]{1,0:T(8,128)(2,1)S(1)}, u32[]{:S(2)}, u32[]{:S(2)}) %collective-permute-start) | collective-permute-done | bytes 98336 | tf_op jit(solution)/shard_map/ppermute | solution.py:392
  33.0 0.3 fusion.1
  33.3 3.3 %collective-permute-start.4 = (bf16[192,256]{1,0:T(8,128)(2,1)S(1)}, bf16[192,256]{1,0:T(8,128)(2,1)S(1)}, u32[]{:S(2)}, u32[]{:S(2)}) collective-permute-start(bf16[192,256]{1,0:T(8,128)(2,1)S(1)} %collective-permute-done.3.refs_4_), channel_id=1, source_target_pairs={{0,56},{8,0},{16,8},{24,16},{32,24},{40,32},{48,40},{56,48},{1,57}... | collective-permute-start | bytes 294920 | tf_op jit(solution)/shard_map/ppermute | solution.py:393
  36.7 2.1 %collective-permute-done.1.refs_2_ = bf16[192,256]{1,0:T(8,128)(2,1)S(1)} collective-permute-done((bf16[192,256]{1,0:T(8,128)(2,1)S(1)}, bf16[192,256]{1,0:T(8,128)(2,1)S(1)}, u32[]{:S(2)}, u32[]{:S(2)}) %collective-permute-start.1) | collective-permute-done | bytes 98336 | tf_op jit(solution)/shard_map/ppermute | solution.py:392
  38.9 3.6 %collective-permute-start.5 = (bf16[192,256]{1,0:T(8,128)(2,1)S(1)}, bf16[192,256]{1,0:T(8,128)(2,1)S(1)}, u32[]{:S(2)}, u32[]{:S(2)}) collective-permute-start(bf16[192,256]{1,0:T(8,128)(2,1)S(1)} %collective-permute-done.4.refs_5_), channel_id=1, source_target_pairs={{0,56},{8,0},{16,8},{24,16},{32,24},{40,32},{48,40},{56,48},{1,57}... | collective-permute-start | bytes 294920 | tf_op jit(solution)/shard_map/ppermute | solution.py:393
  42.5 2.2 %collective-permute-done.2.refs_3_ = bf16[192,256]{1,0:T(8,128)(2,1)S(1)} collective-permute-done((bf16[192,256]{1,0:T(8,128)(2,1)S(1)}, bf16[192,256]{1,0:T(8,128)(2,1)S(1)}, u32[]{:S(2)}, u32[]{:S(2)}) %collective-permute-start.2) | collective-permute-done | bytes 98336 | tf_op jit(solution)/shard_map/ppermute | solution.py:392
  44.7 0.2 fusion.refs_8_
  44.9 5.6 %collective-permute-done.6.refs_7_ = bf16[192,256]{1,0:T(8,128)(2,1)S(1)} collective-permute-done((bf16[192,256]{1,0:T(8,128)(2,1)S(1)}, bf16[192,256]{1,0:T(8,128)(2,1)S(1)}, u32[]{:S(2)}, u32[]{:S(2)}) %collective-permute-start.6) | collective-permute-done | bytes 98336 | tf_op jit(solution)/shard_map/ppermute | solution.py:394
  50.5 0.8 shard_map.66
  51.3 1.3 %copy-done = bf16[32,112,256]{2,1,0:T(8,128)(2,1)} copy-done((bf16[32,112,256]{2,1,0:T(8,128)(2,1)}, bf16[32,112,256]{2,1,0:T(8,128)(2,1)S(1)}, u32[]{:S(2)}) %copy-start) | copy-done | bytes 1835032
  52.5 6.0 %all-to-all-start.1 = ((bf16[32,112,256]{2,1,0:T(8,128)(2,1)}), bf16[32,112,256]{2,1,0:T(8,128)(2,1)S(1)}, u32[]{:S(2)}, u32[]{:S(2)}) async-start(bf16[32,112,256]{2,1,0:T(8,128)(2,1)} %copy-done), calls=%async_computation.1 | async-start | bytes 3670016 | tf_op jit(solution)/shard_map/all_to_all | solution.py:418
  58.5 24.4 %all-to-all-done.1.got_ref = bf16[32,112,256]{2,1,0:T(8,128)(2,1)S(1)} async-done(((bf16[32,112,256]{2,1,0:T(8,128)(2,1)}), bf16[32,112,256]{2,1,0:T(8,128)(2,1)S(1)}, u32[]{:S(2)}, u32[]{:S(2)}) %all-to-all-start.1) | async-done | bytes 1835040 | tf_op jit(solution)/shard_map/all_to_all | solution.py:418
  83.0 14.0 %shard_map.67 = (f32[256,256]{1,0:T(8,128)}, f32[5,128,128]{2,1,0:T(8,128)S(1)}) custom-call(s32[24]{0:T(128)S(1)} %copy-done.1, s32[1]{0:T(128)} %bitcast.base_ref, bf16[24,64,4096]{2,1,0:T(8,128)(2,1)} %tensor_ref.1, bf16[32,112,256]{2,1,0:T(8,128)(2,1)S(1)} %all-to-all-done.1.got_ref), custom_call_target="tpu_custom_call" | custom-call | flops 3221225472 | bytes 12582912 | tf_op jit(solution)/shard_map/pallas_call | solution.py:323
  97.0 3.6 %all-to-all-start.2 = ((f32[4,64,256]{2,1,0:T(8,128)}), f32[4,64,256]{2,1,0:T(8,128)S(1)}, u32[]{:S(2)}, u32[]{:S(2)}) async-start(f32[4,64,256]{2,1,0:T(8,128)} %bitcast.4), calls=%async_computation.2 | async-start | bytes 524288 | tf_op jit(solution)/shard_map/all_to_all | solution.py:421
  100.6 4.4 %shard_map.68.inverse_ref = f32[256,256]{1,0:T(8,128)S(1)} custom-call(f32[5,128,128]{2,1,0:T(8,128)S(1)} %get-tuple-element.8.state_ref), custom_call_target="tpu_custom_call" | custom-call | flops 1000000000 | bytes 1000000 | tf_op jit(solution)/shard_map/pallas_call | solution.py:422
  105.0 2.1 %all-to-all-done.2.parts_ref = f32[4,64,256]{2,1,0:T(8,128)S(1)} async-done(((f32[4,64,256]{2,1,0:T(8,128)}), f32[4,64,256]{2,1,0:T(8,128)S(1)}, u32[]{:S(2)}, u32[]{:S(2)}) %all-to-all-start.2) | async-done | bytes 262176 | tf_op jit(solution)/shard_map/all_to_all | solution.py:421
  107.1 1.4 %shard_map.69 = f32[64,256]{1,0:T(8,128)} custom-call(f32[4,64,256]{2,1,0:T(8,128)S(1)} %all-to-all-done.2.parts_ref, f32[256,256]{1,0:T(8,128)S(1)} %shard_map.68.inverse_ref), custom_call_target="tpu_custom_call" | custom-call | tf_op jit(solution)/shard_map/pallas_call | solution.py:428
  (14 shorter events, 0.2 us)
Async XLA Ops:
  2.8 18.2 %all-to-all-start = ((bf16[32,32,256]{2,1,0:T(8,128)(2,1)}), bf16[32,32,256]{2,1,0:T(8,128)(2,1)S(1)}, u32[]{:S(2)}, u32[]{:S(2)}) async-start(bf16[32,32,256]{2,1,0:T(8,128)(2,1)} %shard_map.64), calls=%async_computation | async-start | bytes 1048576 | tf_op jit(solution)/shard_map/all_to_all | solution.py:381
  21.2 12.1 %collective-permute-start.3 = (bf16[192,256]{1,0:T(8,128)(2,1)S(1)}, bf16[192,256]{1,0:T(8,128)(2,1)S(1)}, u32[]{:S(2)}, u32[]{:S(2)}) collective-permute-start(bf16[192,256]{1,0:T(8,128)(2,1)S(1)} %shard_map.65.refs_0_), channel_id=1, source_target_pairs={{0,56},{8,0},{16,8},{24,16},{32,24},{40,32},{48,40},{56,48},{1,57}... | collective-permute-start | bytes 294920 | tf_op jit(solution)/shard_map/ppermute | solution.py:393
  27.1 5.8 %collective-permute-start = (bf16[192,256]{1,0:T(8,128)(2,1)S(1)}, bf16[192,256]{1,0:T(8,128)(2,1)S(1)}, u32[]{:S(2)}, u32[]{:S(2)}) collective-permute-start(bf16[192,256]{1,0:T(8,128)(2,1)S(1)} %shard_map.65.refs_0_), channel_id=1, source_target_pairs={{0,8},{8,16},{16,24},{24,32},{32,40},{40,48},{48,56},{56,0},{1,9},... | collective-permute-start | bytes 294920 | tf_op jit(solution)/shard_map/ppermute | solution.py:392
  33.0 5.8 %collective-permute-start.1 = (bf16[192,256]{1,0:T(8,128)(2,1)S(1)}, bf16[192,256]{1,0:T(8,128)(2,1)S(1)}, u32[]{:S(2)}, u32[]{:S(2)}) collective-permute-start(bf16[192,256]{1,0:T(8,128)(2,1)S(1)} %collective-permute-done.refs_1_), channel_id=1, source_target_pairs={{0,8},{8,16},{16,24},{24,32},{32,40},{40,48},{48,56},{56,0},{1,9},... | collective-permute-start | bytes 294920 | tf_op jit(solution)/shard_map/ppermute | solution.py:392
  33.3 5.5 %collective-permute-start.4 = (bf16[192,256]{1,0:T(8,128)(2,1)S(1)}, bf16[192,256]{1,0:T(8,128)(2,1)S(1)}, u32[]{:S(2)}, u32[]{:S(2)}) collective-permute-start(bf16[192,256]{1,0:T(8,128)(2,1)S(1)} %collective-permute-done.3.refs_4_), channel_id=1, source_target_pairs={{0,56},{8,0},{16,8},{24,16},{32,24},{40,32},{48,40},{56,48},{1,57}... | collective-permute-start | bytes 294920 | tf_op jit(solution)/shard_map/ppermute | solution.py:393
  38.8 5.8 %collective-permute-start.2 = (bf16[192,256]{1,0:T(8,128)(2,1)S(1)}, bf16[192,256]{1,0:T(8,128)(2,1)S(1)}, u32[]{:S(2)}, u32[]{:S(2)}) collective-permute-start(bf16[192,256]{1,0:T(8,128)(2,1)S(1)} %collective-permute-done.1.refs_2_), channel_id=1, source_target_pairs={{0,8},{8,16},{16,24},{24,32},{32,40},{40,48},{48,56},{56,0},{1,9},... | collective-permute-start | bytes 294920 | tf_op jit(solution)/shard_map/ppermute | solution.py:392
  38.9 6.0 %collective-permute-start.5 = (bf16[192,256]{1,0:T(8,128)(2,1)S(1)}, bf16[192,256]{1,0:T(8,128)(2,1)S(1)}, u32[]{:S(2)}, u32[]{:S(2)}) collective-permute-start(bf16[192,256]{1,0:T(8,128)(2,1)S(1)} %collective-permute-done.4.refs_5_), channel_id=1, source_target_pairs={{0,56},{8,0},{16,8},{24,16},{32,24},{40,32},{48,40},{56,48},{1,57}... | collective-permute-start | bytes 294920 | tf_op jit(solution)/shard_map/ppermute | solution.py:393
  44.6 5.8 %collective-permute-start.6 = (bf16[192,256]{1,0:T(8,128)(2,1)S(1)}, bf16[192,256]{1,0:T(8,128)(2,1)S(1)}, u32[]{:S(2)}, u32[]{:S(2)}) collective-permute-start(bf16[192,256]{1,0:T(8,128)(2,1)S(1)} %collective-permute-done.2.refs_3_), channel_id=1, source_target_pairs={{0,8},{8,16},{16,24},{24,32},{32,40},{40,48},{48,56},{56,0},{1,9},... | collective-permute-start | bytes 294920 | tf_op jit(solution)/shard_map/ppermute | solution.py:394
  51.3 1.3 %copy-start = (bf16[32,112,256]{2,1,0:T(8,128)(2,1)}, bf16[32,112,256]{2,1,0:T(8,128)(2,1)S(1)}, u32[]{:S(2)}) copy-start(bf16[32,112,256]{2,1,0:T(8,128)(2,1)S(1)} %shard_map.66) | copy-start | bytes 5505028
  52.5 30.4 %copy-start.1 = (s32[24]{0:T(128)S(1)}, s32[24]{0:T(128)}, u32[]{:S(2)}) copy-start(s32[24]{0:T(128)} %rows_ref.1) | copy-start | bytes 292
  52.5 30.4 %all-to-all-start.1 = ((bf16[32,112,256]{2,1,0:T(8,128)(2,1)}), bf16[32,112,256]{2,1,0:T(8,128)(2,1)S(1)}, u32[]{:S(2)}, u32[]{:S(2)}) async-start(bf16[32,112,256]{2,1,0:T(8,128)(2,1)} %copy-done), calls=%async_computation.1 | async-start | bytes 3670016 | tf_op jit(solution)/shard_map/all_to_all | solution.py:418
  97.0 10.1 %all-to-all-start.2 = ((f32[4,64,256]{2,1,0:T(8,128)}), f32[4,64,256]{2,1,0:T(8,128)S(1)}, u32[]{:S(2)}, u32[]{:S(2)}) async-start(f32[4,64,256]{2,1,0:T(8,128)} %bitcast.4), calls=%async_computation.2 | async-start | bytes 524288 | tf_op jit(solution)/shard_map/all_to_all | solution.py:421

commit v3 on v2

--- a/solution.py
+++ b/solution.py
@@ -12,7 +12,8 @@
 YS, ZS, CS, XS = 4, 8, 2, 4
 PEERS = YS * CS * XS
 RING = ("y", "c", "x")
-ROWS0 = 32
+PAIRS = YS * CS
+ROWS0 = 48
 ROWS1 = 192
 ROWS2 = 112
 F32 = jnp.float32
@@ -23,12 +24,12 @@
 LIMIT = 48 * 1024 * 1024
 
 
-def call(kernel, out_shape, in_specs, scratch=(), **kw):
+def call(kernel, out_shape, in_specs, scratch=(), out_spec=VMEM, **kw):
     return pl.pallas_call(
         kernel,
         out_shape=out_shape,
         in_specs=in_specs,
-        out_specs=jax.tree.map(lambda _: VMEM, out_shape),
+        out_specs=jax.tree.map(lambda _: out_spec, out_shape),
         scratch_shapes=list(scratch),
         compiler_params=pltpu.CompilerParams(vmem_limit_bytes=LIMIT),
         **kw,
@@ -48,16 +49,16 @@
 
 def put(wide, start, stride, values):
     for half in range(2):
-        wide[half, pl.ds(start, PEERS, stride=stride), :] = values[:, 128 * half : 128 * half + 128]
-
-
-def take(wide, start, stride):
-    return jnp.concatenate([wide[half, pl.ds(start, PEERS, stride=stride), :] for half in range(2)], axis=1)
-
-
-def fill(wide, values):
+        wide[half, pl.ds(start, values.shape[0], stride=stride), :] = values[:, 128 * half : 128 * half + 128]
+
+
+def take(wide, start, stride, count=PEERS):
+    return jnp.concatenate([wide[half, pl.ds(start, count, stride=stride), :] for half in range(2)], axis=1)
+
+
+def fill(wide, values, start=0):
     for half in range(2):
-        wide[half] = values[:, 128 * half : 128 * half + 128]
+        wide[half, start : start + values.shape[0]] = values[:, 128 * half : 128 * half + 128]
 
 
 def whole(wide):
@@ -75,11 +76,11 @@
     return jnp.concatenate([mixed, gram[half:, :half]], axis=1), diagonal
 
 
-def first_kernel(x_ref, second_ref, third_ref, seconds_ref, thirds_ref, out_ref, wide, spot, two, few, at, sems):
+def first_kernel(x_ref, second_ref, third_ref, seconds_ref, thirds_ref, out_ref, wide, table, two, few, at, sems):
     x = x_ref[0]
     copies = [
-        pltpu.make_async_copy(second_ref.at[pl.ds(pl.multiple_of(x * 128, 128), 128), :], two, sems.at[0]),
-        pltpu.make_async_copy(third_ref.at[pl.ds(pl.multiple_of(x * 32, 32), 32), :], few, sems.at[1]),
+        pltpu.make_async_copy(second_ref, two, sems.at[0]),
+        pltpu.make_async_copy(third_ref, few, sems.at[1]),
         pltpu.make_async_copy(seconds_ref, at.at[0], sems.at[2]),
         pltpu.make_async_copy(thirds_ref, at.at[1], sems.at[3]),
     ]
@@ -87,55 +88,76 @@
         copy.start()
     for copy in copies:
         copy.wait()
-    rows_two = two[...]
-    rows_three = few[...]
-    lane = lax.broadcasted_iota(jnp.int32, (PEERS, R), 1)
-    extra = [jnp.zeros((PEERS, R), F32) for _ in range(3)]
-    for which, rows in enumerate((rows_two, rows_three)):
-        packed, diagonal = packed_gram(rows)
-        for part, values in enumerate(three(packed)):
-            for m in range(4):
-                put(wide, 12 * which + 4 * part + m, ROWS0, values[32 * m : 32 * m + 32, :])
-        for part, values in enumerate(three(diagonal)):
-            for m in range(4):
-                extra[part] = jnp.where(
-                    lane == 128 + 4 * which + m, values[32 * m : 32 * m + 32, :], extra[part]
-                )
-    pieces = rows_two.astype(F32)
-    for n in range(4):
-        put(wide, 24 + n, ROWS0, pieces[32 * n : 32 * n + 32, :])
-    put(wide, 28, ROWS0, rows_three.astype(F32))
+
+    def mine(start):
+        return take(table, start + x, XS, PAIRS)
+
+    fill(table, two[...].astype(F32))
+    fill(table, few[...].astype(F32), 512)
+    for n in range(20):
+        put(wide, 24 + n, ROWS0, mine(32 * n))
+    grams = [packed_gram(two[...]), packed_gram(few[...])]
+    lane = lax.broadcasted_iota(jnp.int32, (128, R), 1)
+    column = jnp.where(lane < 132, grams[0][1], grams[1][1])
+    for part, values in enumerate(three(column)):
+        fill(table, values, 128 * part)
+    lane = lane[:PAIRS]
     seconds = at[0]
     names = (seconds >> 4, seconds & 15, at[1])
     for part in range(3):
-        spot[...] = extra[part]
-        spot[:, 0:BLK] = jnp.broadcast_to(names[part].astype(F32), (PEERS, BLK))
-        put(wide, 29 + part, ROWS0, spot[...])
-    out_ref[...] = whole(wide).astype(BF16).reshape(PEERS, ROWS0, R)
-
-
-def second_kernel(got_ref, out_ref, wide, slab):
-    fill(wide, got_ref[...].reshape(PEERS * ROWS0, R).astype(F32))
+        extra = jnp.zeros((PAIRS, R), F32)
+        for m in range(4):
+            extra = jnp.where((lane == 128 + m) | (lane == 132 + m), mine(128 * part + 32 * m), extra)
+        put(wide, 44 + part, ROWS0, extra)
+        wide[0, pl.ds(44 + part, PAIRS, stride=ROWS0), :] = jnp.concatenate(
+            [jnp.broadcast_to(names[part].astype(F32), (PAIRS, BLK)), jnp.zeros((PAIRS, 128 - BLK), F32)], axis=1
+        )
+    put(wide, 47, ROWS0, jnp.zeros((PAIRS, R), F32))
+    for which in range(2):
+        for part, values in enumerate(three(grams[which][0])):
+            fill(table, values, 128 * part)
+            for m in range(4):
+                put(wide, 12 * which + 4 * part + m, ROWS0, mine(128 * part + 32 * m))
+    out_ref[...] = whole(wide).astype(BF16).reshape(PAIRS, ROWS0, R)
+
+
+def second_kernel(z_ref, got_ref, out_ref, places_ref, wide, slab):
+    fill(wide, got_ref[...].reshape(PAIRS * ROWS0, R).astype(F32))
     total = got_ref[0].astype(F32)
-    for source in range(1, PEERS):
+    for source in range(1, PAIRS):
         total = total + got_ref[source].astype(F32)
     for i in range(2):
-        for u in range(2):
-            slab[64 * i + 32 * u : 64 * i + 32 * u + 32, :] = take(wide, 24 + 2 * u + i, ROWS0)
-    slab[128:160, :] = take(wide, 28, ROWS0)
+        for block in range(8):
+            slab[64 * i + 8 * block : 64 * i + 8 * block + 8, :] = take(wide, 24 + 2 * block + i, ROWS0, PAIRS)
+    for n in range(4):
+        slab[128 + 8 * n : 136 + 8 * n, :] = take(wide, 40 + n, ROWS0, PAIRS)
     chunks = [total[12 * w : 12 * w + 4] + total[12 * w + 4 : 12 * w + 8] + total[12 * w + 8 : 12 * w + 12] for w in range(2)]
     for w in range(2):
         for part, values in enumerate(three(chunks[w])):
             slab[160 + 12 * w + 4 * part : 164 + 12 * w + 4 * part, :] = values
     slab[184:192, :] = jnp.zeros((8, R), F32)
-    for part, values in enumerate(three(total[29:30] + total[30:31] + total[31:32])):
+    for part, values in enumerate(three(total[44:45] + total[45:46] + total[46:47])):
         slab[184 + part : 185 + part, :] = values
     out_ref[...] = slab[...].astype(BF16)
 
+    names = [take(wide, 44 + n, ROWS0, PAIRS)[:, :128].astype(jnp.int32) for n in range(3)]
+    seconds, thirds = names[0] * 16 + names[1], names[2]
+
+    def source(holder):
+        back = (z_ref[0] - (holder >> 1)) & (ZS - 1)
+        return ((holder >> 4) << 1) | (holder & 1), jnp.where(back < 4, back, 11 - back)
+
+    pair, plane = source(seconds >> 3)
+    place_two = plane * 64 + (seconds & 7) * PAIRS + pair
+    pair, plane = source(thirds >> 1)
+    place_three = plane * 32 + (thirds & 1) * (2 * PAIRS) + pair
+    places_ref[:PAIRS] = place_two
+    places_ref[PAIRS:] = place_three
+
 
 def third_kernel(*refs):
     pieces = refs[:ZS]
-    pick_two_ref, pick_left_ref, pick_right_ref, out_ref, wide = refs[ZS:]
+    pick_two_ref, pick_left_ref, pick_right_ref, out_ref, wide, narrow, sems = refs[ZS:]
 
     def table(start, stop):
         return jnp.concatenate([ref[start:stop, :] for ref in pieces], axis=0)
@@ -164,7 +186,15 @@
     tail = wide[96:112, :]
     for d in range(1, PEERS):
         wide[d * ROWS2 + 96 : d * ROWS2 + 112, :] = tail
-    out_ref[...] = wide[...].astype(BF16).reshape(PEERS, ROWS2, R)
+    copies = []
+    for n in range(4):
+        peers = pl.ds(8 * n, 8)
+        rows = wide[8 * n * ROWS2 : 8 * (n + 1) * ROWS2, :]
+        narrow[peers] = rows.astype(BF16).reshape(8, ROWS2, R)
+        copies.append(pltpu.make_async_copy(narrow.at[peers], out_ref.at[peers], sems.at[n]))
+        copies[-1].start()
+    for copy in copies:
+        copy.wait()
 
 
 def dot_high(a, b, dims=((1,), (0,))):
@@ -303,9 +333,8 @@
 
     taken = 0
     for t in range(BLK):
-        if t % 4 == 0:
-            for later in range(t, t + 4):
-                fetch(later).wait()
+        for later in range(t, {0: 4, 4: 12, 12: BLK}.get(t, t)):
+            fetch(later).wait()
         one_block(t)
         while taken < min(half // 8, (t + 1) * half // 8 // (BLK - 4)):
             next(steps)
@@ -367,25 +396,26 @@
     keep = functools.partial(pltpu.with_memory_space_constraint, memory_space=pltpu.HBM)
     sent = call(
         first_kernel,
-        shape((PEERS, ROWS0, R), BF16),
+        pltpu.HBM((PAIRS, ROWS0, R), BF16),
         [SMEM, HBM, HBM, HBM, HBM],
         [
-            halves(PEERS * ROWS0),
-            pltpu.VMEM((PEERS, R), F32),
+            halves(PAIRS * ROWS0),
+            halves(640),
+            pltpu.VMEM((512, R), BF16),
             pltpu.VMEM((128, R), BF16),
-            pltpu.VMEM((32, R), BF16),
             pltpu.VMEM((2, 1, BLK), jnp.int32),
             pltpu.SemaphoreType.DMA((4,)),
         ],
     )(x, *map(keep, (second_factor, third_factor, block_seconds.reshape(1, BLK), block_thirds.reshape(1, BLK))))
-    got0 = exchange(sent, RING)
-
-    sent = call(
+    got0 = exchange(sent, ("y", "c"))
+
+    z = lax.axis_index("z").astype(jnp.int32).reshape(1)
+    sent, places = call(
         second_kernel,
-        shape((ROWS1, R), BF16),
-        [VMEM],
-        [halves(PEERS * ROWS0), pltpu.VMEM((ROWS1, R), F32)],
-    )(got0)
+        (shape((ROWS1, R), BF16), shape((2 * PAIRS, 128), jnp.int32)),
+        [SMEM, VMEM],
+        [halves(PAIRS * ROWS0), pltpu.VMEM((ROWS1, R), F32)],
+    )(z, got0)
     around = [[(z, (z + step) % ZS) for z in range(ZS)] for step in (1, -1)]
     from_low, from_high = [sent], [sent]
     for _ in range(3):
@@ -393,28 +423,28 @@
         from_high.append(lax.ppermute(from_high[-1], "z", around[1]))
     pieces = from_low + from_high[1:] + [lax.ppermute(from_low[-1], "z", around[0])]
 
-    names = got0[:, 29:32, :BLK].astype(jnp.int32)
-    seconds = (names[:, 0] * 16 + names[:, 1]).reshape(-1)
-    thirds = names[:, 2].reshape(-1)
-
-    def source(holder):
-        back = (lax.axis_index("z") - holder // CS) % ZS
-        return (holder // (ZS * CS)) * CS + holder % CS, jnp.where(back < 4, back, 11 - back)
-
-    pair, plane = source(seconds // 8)
-    place_two = plane * 64 + seconds % 2 * 32 + pair * XS + seconds % 8 // 2
-    pair, plane = source(thirds // 2)
-    place_three = plane * 32 + pair * XS + thirds % 2 * 2
+    others = [
+        lax.ppermute(places, "x", [(n, (n + step) % XS) for n in range(XS)]) for step in (3, 2, 1)
+    ]
+    places = jnp.stack([*others, places] * 2)
+    places = lax.dynamic_slice_in_dim(places, XS - 1 - lax.axis_index("x"), XS, 0)[:, :, :BLK]
+    place_two = places[:, :PAIRS].swapaxes(0, 1).reshape(-1)
+    place_three = places[:, PAIRS:].swapaxes(0, 1).reshape(-1)
 
     def one_hot(place, width):
         return (place[:, None] == jnp.arange(width)[None, :]).astype(BF16)
 
     sent = call(
         third_kernel,
-        shape((PEERS, ROWS2, R), BF16),
+        pltpu.HBM((PEERS, ROWS2, R), BF16),
         [VMEM] * (ZS + 3),
-        [pltpu.VMEM((PEERS * ROWS2, R), F32)],
-    )(*pieces, one_hot(place_two, 64 * ZS), one_hot(place_three, 32 * ZS), one_hot(place_three + 1, 32 * ZS))
+        [
+            pltpu.VMEM((PEERS * ROWS2, R), F32),
+            pltpu.VMEM((PEERS, ROWS2, R), BF16),
+            pltpu.SemaphoreType.DMA((4,)),
+        ],
+        HBM,
+    )(*pieces, one_hot(place_two, 64 * ZS), one_hot(place_three, 32 * ZS), one_hot(place_three + PAIRS, 32 * ZS))
     got2 = exchange(sent, RING)
 
     summed, state = products(block_rows, base, tensor_blocks, got2)

time: 109 us -> 105 us (0.963)
  waiting for transfers between devices: 52.6 us -> 48.8 us
  starting transfers between devices: 30 us -> 31.4 us
  local copies, waits for them, and re-layouts: 1.42 us -> 0.23 us
    all_to_all x1, waiting for transfers between devices: 10.6 us -> 5.41 us  [body(): got0 = exchange(sent, ('y', 'c'))]
    ppermute x0 -> x3, starting transfers between devices: none -> 4.53 us  [body(): lax.ppermute(places, 'x', [(n, (n + step) % XS) for n in range(XS)])]
    all_to_all x1, starting transfers between devices: 7.55 us -> 5.5 us  [body(): got0 = exchange(sent, ('y', 'c'))]
    ppermute x3, waiting for transfers between devices: 9.86 us -> 11.2 us  [body(): from_low.append(lax.ppermute(from_low[-1], 'z', around[0]))]
    unnamed x4 -> x9, local copies, waits for them, and re-layouts: 1.26 us -> 0.03 us
  transfers between devices with their start and end apart: 10 -> 13, of which waited for: 7 -> 7; matrix products, arithmetic and copies ran while one was open for 1% -> 1% of each run, Pallas kernels for 4% -> 4%
where the time goes in v3:
time: 105 us
  waiting for transfers between devices  48.8 us (46%)
  starting transfers between devices  31.4 us (30%)
  Pallas kernels  23.6 us (22%)
    all_to_all x1, waiting for transfers between devices, body(): got2 = exchange(sent, RING)  24.4 us
    pallas_call x1, Pallas kernels, products(): call(product_kernel, (jax.ShapeDtypeStruct((XS * BS, R), F32), jax.ShapeD...  13.5 us
    ppermute x3, starting transfers between devices, body(): from_high.append(lax.ppermute(from_high[-1], 'z', around[1]))  12.4 us
    ppermute x3, waiting for transfers between devices, body(): from_low.append(lax.ppermute(from_low[-1], 'z', around[0]))  11.2 us
    ppermute x1, waiting for transfers between devices, body(): lax.ppermute(from_low[-1], 'z', around[0])  5.61 us
    all_to_all x1, starting transfers between devices, body(): got0 = exchange(sent, ('y', 'c'))  5.5 us
    all_to_all x1, waiting for transfers between devices, body(): got0 = exchange(sent, ('y', 'c'))  5.41 us
    all_to_all x1, starting transfers between devices, body(): got2 = exchange(sent, RING)  5.32 us
  transfers between devices with their start and end apart: 13, of which 7 were waited for; matrix products, arithmetic and copies ran while one was open for 1% of the time, Pallas kernels for 4%

profile of v3, /device:TPU:8, one launch (start us, length us, event | category | flops | bytes accessed | tf_op | source)
XLA Modules:
  0.0 104.7 jit_solution(9319788110699648526)
XLA Ops:
  0.0 2.3 %shard_map.64 = bf16[8,48,256]{2,1,0:T(8,128)(2,1)} custom-call(s32[1]{0:T(128)} %bitcast.2.x_ref, bf16[512,256]{1,0:T(8,128)(2,1)} %second_ref.1, bf16[128,256]{1,0:T(8,128)(2,1)} %third_ref.1, s32[1,24]{1,0:T(1,128)} %bitcast.22, s32[1,24]{1,0:T(1,128)} %bitcast.23), custom_call_target="tpu_custom_call" | custom-call | tf_op jit(solution)/shard_map/pallas_call | solution.py:397
  2.3 5.5 %all-to-all-start = ((bf16[8,48,256]{2,1,0:T(8,128)(2,1)}), bf16[8,48,256]{2,1,0:T(8,128)(2,1)S(1)}, u32[]{:S(2)}, u32[]{:S(2)}) async-start(bf16[8,48,256]{2,1,0:T(8,128)(2,1)} %shard_map.64), calls=%async_computation | async-start | bytes 393216 | tf_op jit(solution)/shard_map/all_to_all | solution.py:410
  7.8 5.4 %all-to-all-done.got_ref = bf16[8,48,256]{2,1,0:T(8,128)(2,1)S(1)} async-done(((bf16[8,48,256]{2,1,0:T(8,128)(2,1)}), bf16[8,48,256]{2,1,0:T(8,128)(2,1)S(1)}, u32[]{:S(2)}, u32[]{:S(2)}) %all-to-all-start) | async-done | bytes 196640 | tf_op jit(solution)/shard_map/all_to_all | solution.py:410
  13.2 0.1 shard_map.65
  13.3 2.2 %collective-permute-start.7 = (s32[16,128]{1,0:T(8,128)S(1)}, s32[16,128]{1,0:T(8,128)S(1)}, u32[]{:S(2)}, u32[]{:S(2)}) collective-permute-start(s32[16,128]{1,0:T(8,128)S(1)} %get-tuple-element.10), channel_id=1, source_target_pairs={{0,3},{1,0},{2,1},{3,2},{4,7},{5,4},{6,5},{7,6},{8,11},{9,8},{10,9... | collective-permute-start | bytes 24584 | tf_op jit(solution)/shard_map/ppermute | solution.py:427
  15.5 2.3 %collective-permute-start.8 = (s32[16,128]{1,0:T(8,128)S(1)}, s32[16,128]{1,0:T(8,128)S(1)}, u32[]{:S(2)}, u32[]{:S(2)}) collective-permute-start(s32[16,128]{1,0:T(8,128)S(1)} %get-tuple-element.10), channel_id=1, source_target_pairs={{0,2},{1,3},{2,0},{3,1},{4,6},{5,7},{6,4},{7,5},{8,10},{9,11},{10,... | collective-permute-start | bytes 24584 | tf_op jit(solution)/shard_map/ppermute | solution.py:427
  17.8 5.9 %collective-permute-start.3 = (bf16[192,256]{1,0:T(8,128)(2,1)S(1)}, bf16[192,256]{1,0:T(8,128)(2,1)S(1)}, u32[]{:S(2)}, u32[]{:S(2)}) collective-permute-start(bf16[192,256]{1,0:T(8,128)(2,1)S(1)} %get-tuple-element.9.refs_0_), channel_id=1, source_target_pairs={{0,56},{8,0},{16,8},{24,16},{32,24},{40,32},{48,40},{56,48},{1,57}... | collective-permute-start | bytes 294920 | tf_op jit(solution)/shard_map/ppermute | solution.py:423
  23.8 0.1 eq.47
  23.9 5.6 %collective-permute-done.refs_1_ = bf16[192,256]{1,0:T(8,128)(2,1)S(1)} collective-permute-done((bf16[192,256]{1,0:T(8,128)(2,1)S(1)}, bf16[192,256]{1,0:T(8,128)(2,1)S(1)}, u32[]{:S(2)}, u32[]{:S(2)}) %collective-permute-start) | collective-permute-done | bytes 98336 | tf_op jit(solution)/shard_map/ppermute | solution.py:422
  29.5 3.2 %collective-permute-start.4 = (bf16[192,256]{1,0:T(8,128)(2,1)S(1)}, bf16[192,256]{1,0:T(8,128)(2,1)S(1)}, u32[]{:S(2)}, u32[]{:S(2)}) collective-permute-start(bf16[192,256]{1,0:T(8,128)(2,1)S(1)} %collective-permute-done.3.refs_4_), channel_id=1, source_target_pairs={{0,56},{8,0},{16,8},{24,16},{32,24},{40,32},{48,40},{56,48},{1,57}... | collective-permute-start | bytes 294920 | tf_op jit(solution)/shard_map/ppermute | solution.py:423
  32.7 2.6 %collective-permute-done.1.refs_2_ = bf16[192,256]{1,0:T(8,128)(2,1)S(1)} collective-permute-done((bf16[192,256]{1,0:T(8,128)(2,1)S(1)}, bf16[192,256]{1,0:T(8,128)(2,1)S(1)}, u32[]{:S(2)}, u32[]{:S(2)}) %collective-permute-start.1) | collective-permute-done | bytes 98336 | tf_op jit(solution)/shard_map/ppermute | solution.py:422
  35.4 0.3 fusion.1
  35.8 3.3 %collective-permute-start.5 = (bf16[192,256]{1,0:T(8,128)(2,1)S(1)}, bf16[192,256]{1,0:T(8,128)(2,1)S(1)}, u32[]{:S(2)}, u32[]{:S(2)}) collective-permute-start(bf16[192,256]{1,0:T(8,128)(2,1)S(1)} %collective-permute-done.4.refs_5_), channel_id=1, source_target_pairs={{0,56},{8,0},{16,8},{24,16},{32,24},{40,32},{48,40},{56,48},{1,57}... | collective-permute-start | bytes 294920 | tf_op jit(solution)/shard_map/ppermute | solution.py:423
  39.1 3.0 %collective-permute-done.2.refs_3_ = bf16[192,256]{1,0:T(8,128)(2,1)S(1)} collective-permute-done((bf16[192,256]{1,0:T(8,128)(2,1)S(1)}, bf16[192,256]{1,0:T(8,128)(2,1)S(1)}, u32[]{:S(2)}, u32[]{:S(2)}) %collective-permute-start.2) | collective-permute-done | bytes 98336 | tf_op jit(solution)/shard_map/ppermute | solution.py:422
  42.1 0.2 fusion.refs_8_
  42.3 5.6 %collective-permute-done.6.refs_7_ = bf16[192,256]{1,0:T(8,128)(2,1)S(1)} collective-permute-done((bf16[192,256]{1,0:T(8,128)(2,1)S(1)}, bf16[192,256]{1,0:T(8,128)(2,1)S(1)}, u32[]{:S(2)}, u32[]{:S(2)}) %collective-permute-start.6) | collective-permute-done | bytes 98336 | tf_op jit(solution)/shard_map/ppermute | solution.py:424
  47.9 1.9 %shard_map.66 = bf16[32,112,256]{2,1,0:T(8,128)(2,1)} custom-call(bf16[192,256]{1,0:T(8,128)(2,1)S(1)} %get-tuple-element.9.refs_0_, bf16[192,256]{1,0:T(8,128)(2,1)S(1)} %collective-permute-done.refs_1_, bf16[192,256]{1,0:T(8,128)(2,1)S(1)} %collective-permute-done.1.refs_2_, bf16[192,256]{1,0:T(8,128)(2,1)S(1)} %collective-permute-done.2.refs_3_, ...), custom_call_target="tpu_custom_call" | custom-call | tf_op jit(solution)/shard_map/pallas_call | solution.py:437
  49.9 5.3 %all-to-all-start.1 = ((bf16[32,112,256]{2,1,0:T(8,128)(2,1)}), bf16[32,112,256]{2,1,0:T(8,128)(2,1)S(1)}, u32[]{:S(2)}, u32[]{:S(2)}) async-start(bf16[32,112,256]{2,1,0:T(8,128)(2,1)} %shard_map.66), calls=%async_computation.1 | async-start | bytes 3670016 | tf_op jit(solution)/shard_map/all_to_all | solution.py:448
  55.2 24.4 %all-to-all-done.1.got_ref = bf16[32,112,256]{2,1,0:T(8,128)(2,1)S(1)} async-done(((bf16[32,112,256]{2,1,0:T(8,128)(2,1)}), bf16[32,112,256]{2,1,0:T(8,128)(2,1)S(1)}, u32[]{:S(2)}, u32[]{:S(2)}) %all-to-all-start.1) | async-done | bytes 1835040 | tf_op jit(solution)/shard_map/all_to_all | solution.py:448
  79.7 13.5 %shard_map.67 = (f32[256,256]{1,0:T(8,128)}, f32[5,128,128]{2,1,0:T(8,128)S(1)}) custom-call(s32[24]{0:T(128)S(1)} %copy-done, s32[1]{0:T(128)} %bitcast.base_ref, bf16[24,64,4096]{2,1,0:T(8,128)(2,1)} %tensor_ref.1, bf16[32,112,256]{2,1,0:T(8,128)(2,1)S(1)} %all-to-all-done.1.got_ref), custom_call_target="tpu_custom_call" | custom-call | flops 3221225472 | bytes 12582912 | tf_op jit(solution)/shard_map/pallas_call | solution.py:352
  93.2 3.6 %all-to-all-start.2 = ((f32[4,64,256]{2,1,0:T(8,128)}), f32[4,64,256]{2,1,0:T(8,128)S(1)}, u32[]{:S(2)}, u32[]{:S(2)}) async-start(f32[4,64,256]{2,1,0:T(8,128)} %bitcast.11), calls=%async_computation.2 | async-start | bytes 524288 | tf_op jit(solution)/shard_map/all_to_all | solution.py:451
  96.8 4.4 %shard_map.68.inverse_ref = f32[256,256]{1,0:T(8,128)S(1)} custom-call(f32[5,128,128]{2,1,0:T(8,128)S(1)} %get-tuple-element.12.state_ref), custom_call_target="tpu_custom_call" | custom-call | flops 1000000000 | bytes 1000000 | tf_op jit(solution)/shard_map/pallas_call | solution.py:452
  101.2 2.1 %all-to-all-done.2.parts_ref = f32[4,64,256]{2,1,0:T(8,128)S(1)} async-done(((f32[4,64,256]{2,1,0:T(8,128)}), f32[4,64,256]{2,1,0:T(8,128)S(1)}, u32[]{:S(2)}, u32[]{:S(2)}) %all-to-all-start.2) | async-done | bytes 262176 | tf_op jit(solution)/shard_map/all_to_all | solution.py:451
  103.3 1.4 %shard_map.69 = f32[64,256]{1,0:T(8,128)} custom-call(f32[4,64,256]{2,1,0:T(8,128)S(1)} %all-to-all-done.2.parts_ref, f32[256,256]{1,0:T(8,128)S(1)} %shard_map.68.inverse_ref), custom_call_target="tpu_custom_call" | custom-call | tf_op jit(solution)/shard_map/pallas_call | solution.py:458
  (26 shorter events, 0.2 us)
Async XLA Ops:
  2.3 10.9 %all-to-all-start = ((bf16[8,48,256]{2,1,0:T(8,128)(2,1)}), bf16[8,48,256]{2,1,0:T(8,128)(2,1)S(1)}, u32[]{:S(2)}, u32[]{:S(2)}) async-start(bf16[8,48,256]{2,1,0:T(8,128)(2,1)} %shard_map.64), calls=%async_computation | async-start | bytes 393216 | tf_op jit(solution)/shard_map/all_to_all | solution.py:410
  13.3 10.4 %collective-permute-start.7 = (s32[16,128]{1,0:T(8,128)S(1)}, s32[16,128]{1,0:T(8,128)S(1)}, u32[]{:S(2)}, u32[]{:S(2)}) collective-permute-start(s32[16,128]{1,0:T(8,128)S(1)} %get-tuple-element.10), channel_id=1, source_target_pairs={{0,3},{1,0},{2,1},{3,2},{4,7},{5,4},{6,5},{7,6},{8,11},{9,8},{10,9... | collective-permute-start | bytes 24584 | tf_op jit(solution)/shard_map/ppermute | solution.py:427
  15.5 8.2 %collective-permute-start.9 = (s32[16,128]{1,0:T(8,128)S(1)}, s32[16,128]{1,0:T(8,128)S(1)}, u32[]{:S(2)}, u32[]{:S(2)}) collective-permute-start(s32[16,128]{1,0:T(8,128)S(1)} %get-tuple-element.10), channel_id=1, source_target_pairs={{0,1},{1,2},{2,3},{3,0},{4,5},{5,6},{6,7},{7,4},{8,9},{9,10},{10,1... | collective-permute-start | bytes 24584 | tf_op jit(solution)/shard_map/ppermute | solution.py:427
  15.5 8.2 %collective-permute-start.8 = (s32[16,128]{1,0:T(8,128)S(1)}, s32[16,128]{1,0:T(8,128)S(1)}, u32[]{:S(2)}, u32[]{:S(2)}) collective-permute-start(s32[16,128]{1,0:T(8,128)S(1)} %get-tuple-element.10), channel_id=1, source_target_pairs={{0,2},{1,3},{2,0},{3,1},{4,6},{5,7},{6,4},{7,5},{8,10},{9,11},{10,... | collective-permute-start | bytes 24584 | tf_op jit(solution)/shard_map/ppermute | solution.py:427
  17.8 11.7 %collective-permute-start.3 = (bf16[192,256]{1,0:T(8,128)(2,1)S(1)}, bf16[192,256]{1,0:T(8,128)(2,1)S(1)}, u32[]{:S(2)}, u32[]{:S(2)}) collective-permute-start(bf16[192,256]{1,0:T(8,128)(2,1)S(1)} %get-tuple-element.9.refs_0_), channel_id=1, source_target_pairs={{0,56},{8,0},{16,8},{24,16},{32,24},{40,32},{48,40},{56,48},{1,57}... | collective-permute-start | bytes 294920 | tf_op jit(solution)/shard_map/ppermute | solution.py:423
  23.7 5.8 %collective-permute-start = (bf16[192,256]{1,0:T(8,128)(2,1)S(1)}, bf16[192,256]{1,0:T(8,128)(2,1)S(1)}, u32[]{:S(2)}, u32[]{:S(2)}) collective-permute-start(bf16[192,256]{1,0:T(8,128)(2,1)S(1)} %get-tuple-element.9.refs_0_), channel_id=1, source_target_pairs={{0,8},{8,16},{16,24},{24,32},{32,40},{40,48},{48,56},{56,0},{1,9},... | collective-permute-start | bytes 294920 | tf_op jit(solution)/shard_map/ppermute | solution.py:422
  29.5 5.9 %collective-permute-start.1 = (bf16[192,256]{1,0:T(8,128)(2,1)S(1)}, bf16[192,256]{1,0:T(8,128)(2,1)S(1)}, u32[]{:S(2)}, u32[]{:S(2)}) collective-permute-start(bf16[192,256]{1,0:T(8,128)(2,1)S(1)} %collective-permute-done.refs_1_), channel_id=1, source_target_pairs={{0,8},{8,16},{16,24},{24,32},{32,40},{40,48},{48,56},{56,0},{1,9},... | collective-permute-start | bytes 294920 | tf_op jit(solution)/shard_map/ppermute | solution.py:422
  29.5 6.3 %collective-permute-start.4 = (bf16[192,256]{1,0:T(8,128)(2,1)S(1)}, bf16[192,256]{1,0:T(8,128)(2,1)S(1)}, u32[]{:S(2)}, u32[]{:S(2)}) collective-permute-start(bf16[192,256]{1,0:T(8,128)(2,1)S(1)} %collective-permute-done.3.refs_4_), channel_id=1, source_target_pairs={{0,56},{8,0},{16,8},{24,16},{32,24},{40,32},{48,40},{56,48},{1,57}... | collective-permute-start | bytes 294920 | tf_op jit(solution)/shard_map/ppermute | solution.py:423
  35.4 6.7 %collective-permute-start.2 = (bf16[192,256]{1,0:T(8,128)(2,1)S(1)}, bf16[192,256]{1,0:T(8,128)(2,1)S(1)}, u32[]{:S(2)}, u32[]{:S(2)}) collective-permute-start(bf16[192,256]{1,0:T(8,128)(2,1)S(1)} %collective-permute-done.1.refs_2_), channel_id=1, source_target_pairs={{0,8},{8,16},{16,24},{24,32},{32,40},{40,48},{48,56},{56,0},{1,9},... | collective-permute-start | bytes 294920 | tf_op jit(solution)/shard_map/ppermute | solution.py:422
  35.8 6.5 %collective-permute-start.5 = (bf16[192,256]{1,0:T(8,128)(2,1)S(1)}, bf16[192,256]{1,0:T(8,128)(2,1)S(1)}, u32[]{:S(2)}, u32[]{:S(2)}) collective-permute-start(bf16[192,256]{1,0:T(8,128)(2,1)S(1)} %collective-permute-done.4.refs_5_), channel_id=1, source_target_pairs={{0,56},{8,0},{16,8},{24,16},{32,24},{40,32},{48,40},{56,48},{1,57}... | collective-permute-start | bytes 294920 | tf_op jit(solution)/shard_map/ppermute | solution.py:423
  42.1 5.8 %collective-permute-start.6 = (bf16[192,256]{1,0:T(8,128)(2,1)S(1)}, bf16[192,256]{1,0:T(8,128)(2,1)S(1)}, u32[]{:S(2)}, u32[]{:S(2)}) collective-permute-start(bf16[192,256]{1,0:T(8,128)(2,1)S(1)} %collective-permute-done.2.refs_3_), channel_id=1, source_target_pairs={{0,8},{8,16},{16,24},{24,32},{32,40},{40,48},{48,56},{56,0},{1,9},... | collective-permute-start | bytes 294920 | tf_op jit(solution)/shard_map/ppermute | solution.py:424
  49.9 29.8 %copy-start = (s32[24]{0:T(128)S(1)}, s32[24]{0:T(128)}, u32[]{:S(2)}) copy-start(s32[24]{0:T(128)} %rows_ref.1) | copy-start | bytes 292
  49.9 29.8 %all-to-all-start.1 = ((bf16[32,112,256]{2,1,0:T(8,128)(2,1)}), bf16[32,112,256]{2,1,0:T(8,128)(2,1)S(1)}, u32[]{:S(2)}, u32[]{:S(2)}) async-start(bf16[32,112,256]{2,1,0:T(8,128)(2,1)} %shard_map.66), calls=%async_computation.1 | async-start | bytes 3670016 | tf_op jit(solution)/shard_map/all_to_all | solution.py:448
  93.2 10.1 %all-to-all-start.2 = ((f32[4,64,256]{2,1,0:T(8,128)}), f32[4,64,256]{2,1,0:T(8,128)S(1)}, u32[]{:S(2)}, u32[]{:S(2)}) async-start(f32[4,64,256]{2,1,0:T(8,128)} %bitcast.11), calls=%async_computation.2 | async-start | bytes 524288 | tf_op jit(solution)/shard_map/all_to_all | solution.py:451

commit v4 on v3

--- a/solution.py
+++ b/solution.py
@@ -343,7 +343,7 @@
     lower = dot_high(below, first, ((1,), (1,)))
     state_ref[0] = first
     state_ref[1] = corner - dot_high(lower, lower, ((1,), (1,)))
-    state_ref[2] = dot_high(lower, first)
+    state_ref[2] = lower
     state_ref[3] = jnp.broadcast_to(scale, (half, half))
     state_ref[4] = jnp.broadcast_to(scale_last, (half, half))
 
@@ -372,10 +372,12 @@
     down = lax.broadcasted_iota(jnp.int32, (half, half), 0)
     along = lax.broadcasted_iota(jnp.int32, (half, half), 1)
     scale, scale_last = state_ref[3, :1], state_ref[4, :1]
+    first = state_ref[0]
+    middle = dot_high(state_ref[2], first)
     last = finish(eliminate(state_ref[1], down, along))
-    out_ref[:half, :half] = state_ref[0] * scale
+    out_ref[:half, :half] = first * scale
     out_ref[:half, half:] = jnp.zeros((half, half), F32)
-    out_ref[half:, :half] = -dot_high(last, state_ref[2]) * scale
+    out_ref[half:, :half] = -dot_high(last, middle) * scale
     out_ref[half:, half:] = last * scale_last
 
 
@@ -421,8 +423,9 @@
     for _ in range(3):
         from_low.append(lax.ppermute(from_low[-1], "z", around[0]))
         from_high.append(lax.ppermute(from_high[-1], "z", around[1]))
-    pieces = from_low + from_high[1:] + [lax.ppermute(from_low[-1], "z", around[0])]
-
+    pieces = from_low + from_high[1:] + [lax.ppermute(from_high[-1], "z", around[1])]
+
+    places, _ = lax.optimization_barrier((places, from_high[2]))
     others = [
         lax.ppermute(places, "x", [(n, (n + step) % XS) for n in range(XS)]) for step in (3, 2, 1)
     ]

time: 105 us -> 101 us (0.962)
  waiting for transfers between devices: 48.8 us -> 40.7 us
  starting transfers between devices: 31.4 us -> 35.8 us
    ppermute x3, waiting for transfers between devices: 11.2 us -> 0.01 us  [body(): from_low.append(lax.ppermute(from_low[-1], 'z', around[0]))]
    ppermute x3, waiting for transfers between devices: 0.01 us -> 6.83 us  [body(): from_high.append(lax.ppermute(from_high[-1], 'z', around[1]))]
    ppermute x1, starting transfers between devices: 0.01 us -> 3.69 us  [body(): lax.ppermute(from_high[-1], 'z', around[1])]
    ppermute x1, waiting for transfers between devices: 5.61 us -> 2 us  [body(): lax.ppermute(from_high[-1], 'z', around[1])]
where the time goes in v4:
time: 101 us
  waiting for transfers between devices  40.7 us (40%)
  starting transfers between devices  35.8 us (35%)
  Pallas kernels  23.7 us (23%)
    all_to_all x1, waiting for transfers between devices, body(): got2 = exchange(sent, RING)  24.4 us
    pallas_call x1, Pallas kernels, products(): call(product_kernel, (jax.ShapeDtypeStruct((XS * BS, R), F32), jax.ShapeD...  13.5 us
    ppermute x3, starting transfers between devices, body(): from_high.append(lax.ppermute(from_high[-1], 'z', around[1]))  12.6 us
    ppermute x3, waiting for transfers between devices, body(): from_high.append(lax.ppermute(from_high[-1], 'z', around[1]))  6.83 us
    all_to_all x1, starting transfers between devices, body(): got0 = exchange(sent, ('y', 'c'))  5.5 us
    all_to_all x1, waiting for transfers between devices, body(): got0 = exchange(sent, ('y', 'c'))  5.41 us
    all_to_all x1, starting transfers between devices, body(): got2 = exchange(sent, RING)  5.32 us
    ppermute x3, starting transfers between devices, body(): lax.ppermute(places, 'x', [(n, (n + step) % XS) for n in range(XS)])  5.05 us
  transfers between devices with their start and end apart: 13, of which 7 were waited for; matrix products, arithmetic and copies ran while one was open for 1% of the time, Pallas kernels for 4%

profile of v4, /device:TPU:8, one launch (start us, length us, event | category | flops | bytes accessed | tf_op | source)
XLA Modules:
  0.0 101.1 jit_solution(2566099871575716085)
XLA Ops:
  0.0 2.3 %shard_map.64 = bf16[8,48,256]{2,1,0:T(8,128)(2,1)} custom-call(s32[1]{0:T(128)} %bitcast.2.x_ref, bf16[512,256]{1,0:T(8,128)(2,1)} %second_ref.1, bf16[128,256]{1,0:T(8,128)(2,1)} %third_ref.1, s32[1,24]{1,0:T(1,128)} %bitcast.22, s32[1,24]{1,0:T(1,128)} %bitcast.23), custom_call_target="tpu_custom_call" | custom-call | tf_op jit(solution)/shard_map/pallas_call | solution.py:399
  2.3 5.5 %all-to-all-start = ((bf16[8,48,256]{2,1,0:T(8,128)(2,1)}), bf16[8,48,256]{2,1,0:T(8,128)(2,1)S(1)}, u32[]{:S(2)}, u32[]{:S(2)}) async-start(bf16[8,48,256]{2,1,0:T(8,128)(2,1)} %shard_map.64), calls=%async_computation | async-start | bytes 393216 | tf_op jit(solution)/shard_map/all_to_all | solution.py:412
  7.8 5.4 %all-to-all-done.got_ref = bf16[8,48,256]{2,1,0:T(8,128)(2,1)S(1)} async-done(((bf16[8,48,256]{2,1,0:T(8,128)(2,1)}), bf16[8,48,256]{2,1,0:T(8,128)(2,1)S(1)}, u32[]{:S(2)}, u32[]{:S(2)}) %all-to-all-start) | async-done | bytes 196640 | tf_op jit(solution)/shard_map/all_to_all | solution.py:412
  13.2 0.1 shard_map.65
  13.3 5.3 %collective-permute-start.3 = (bf16[192,256]{1,0:T(8,128)(2,1)S(1)}, bf16[192,256]{1,0:T(8,128)(2,1)S(1)}, u32[]{:S(2)}, u32[]{:S(2)}) collective-permute-start(bf16[192,256]{1,0:T(8,128)(2,1)S(1)} %get-tuple-element.10.refs_0_), channel_id=1, source_target_pairs={{0,56},{8,0},{16,8},{24,16},{32,24},{40,32},{48,40},{56,48},{1,57}... | collective-permute-start | bytes 294920 | tf_op jit(solution)/shard_map/ppermute | solution.py:425
  18.6 2.2 %collective-permute-done.3.refs_4_ = bf16[192,256]{1,0:T(8,128)(2,1)S(1)} collective-permute-done((bf16[192,256]{1,0:T(8,128)(2,1)S(1)}, bf16[192,256]{1,0:T(8,128)(2,1)S(1)}, u32[]{:S(2)}, u32[]{:S(2)}) %collective-permute-start.3) | collective-permute-done | bytes 98336 | tf_op jit(solution)/shard_map/ppermute | solution.py:425
  20.8 3.6 %collective-permute-start.4 = (bf16[192,256]{1,0:T(8,128)(2,1)S(1)}, bf16[192,256]{1,0:T(8,128)(2,1)S(1)}, u32[]{:S(2)}, u32[]{:S(2)}) collective-permute-start(bf16[192,256]{1,0:T(8,128)(2,1)S(1)} %collective-permute-done.3.refs_4_), channel_id=1, source_target_pairs={{0,56},{8,0},{16,8},{24,16},{32,24},{40,32},{48,40},{56,48},{1,57}... | collective-permute-start | bytes 294920 | tf_op jit(solution)/shard_map/ppermute | solution.py:425
  24.5 2.2 %collective-permute-done.4.refs_5_ = bf16[192,256]{1,0:T(8,128)(2,1)S(1)} collective-permute-done((bf16[192,256]{1,0:T(8,128)(2,1)S(1)}, bf16[192,256]{1,0:T(8,128)(2,1)S(1)}, u32[]{:S(2)}, u32[]{:S(2)}) %collective-permute-start.4) | collective-permute-done | bytes 98336 | tf_op jit(solution)/shard_map/ppermute | solution.py:425
  26.7 2.8 %collective-permute-start.7 = (s32[16,128]{1,0:T(8,128)S(1)}, s32[16,128]{1,0:T(8,128)S(1)}, u32[]{:S(2)}, u32[]{:S(2)}) collective-permute-start(s32[16,128]{1,0:T(8,128)S(1)} %get-tuple-element.12), channel_id=1, source_target_pairs={{0,3},{1,0},{2,1},{3,2},{4,7},{5,4},{6,5},{7,6},{8,11},{9,8},{10,9... | collective-permute-start | bytes 24584 | tf_op jit(solution)/shard_map/ppermute | solution.py:430
  29.4 2.3 %collective-permute-start.8 = (s32[16,128]{1,0:T(8,128)S(1)}, s32[16,128]{1,0:T(8,128)S(1)}, u32[]{:S(2)}, u32[]{:S(2)}) collective-permute-start(s32[16,128]{1,0:T(8,128)S(1)} %get-tuple-element.12), channel_id=1, source_target_pairs={{0,2},{1,3},{2,0},{3,1},{4,6},{5,7},{6,4},{7,5},{8,10},{9,11},{10,... | collective-permute-start | bytes 24584 | tf_op jit(solution)/shard_map/ppermute | solution.py:430
  31.7 3.6 %collective-permute-start.5 = (bf16[192,256]{1,0:T(8,128)(2,1)S(1)}, bf16[192,256]{1,0:T(8,128)(2,1)S(1)}, u32[]{:S(2)}, u32[]{:S(2)}) collective-permute-start(bf16[192,256]{1,0:T(8,128)(2,1)S(1)} %collective-permute-done.4.refs_5_), channel_id=1, source_target_pairs={{0,56},{8,0},{16,8},{24,16},{32,24},{40,32},{48,40},{56,48},{1,57}... | collective-permute-start | bytes 294920 | tf_op jit(solution)/shard_map/ppermute | solution.py:425
  35.6 0.3 fusion.1
  36.0 2.4 %collective-permute-done.5.refs_6_ = bf16[192,256]{1,0:T(8,128)(2,1)S(1)} collective-permute-done((bf16[192,256]{1,0:T(8,128)(2,1)S(1)}, bf16[192,256]{1,0:T(8,128)(2,1)S(1)}, u32[]{:S(2)}, u32[]{:S(2)}) %collective-permute-start.5) | collective-permute-done | bytes 98336 | tf_op jit(solution)/shard_map/ppermute | solution.py:425
  38.4 3.7 %collective-permute-start.6 = (bf16[192,256]{1,0:T(8,128)(2,1)S(1)}, bf16[192,256]{1,0:T(8,128)(2,1)S(1)}, u32[]{:S(2)}, u32[]{:S(2)}) collective-permute-start(bf16[192,256]{1,0:T(8,128)(2,1)S(1)} %collective-permute-done.5.refs_6_), channel_id=1, source_target_pairs={{0,56},{8,0},{16,8},{24,16},{32,24},{40,32},{48,40},{56,48},{1,57}... | collective-permute-start | bytes 294920 | tf_op jit(solution)/shard_map/ppermute | solution.py:426
  42.1 0.2 fusion.refs_8_
  42.3 2.0 %collective-permute-done.6.refs_7_ = bf16[192,256]{1,0:T(8,128)(2,1)S(1)} collective-permute-done((bf16[192,256]{1,0:T(8,128)(2,1)S(1)}, bf16[192,256]{1,0:T(8,128)(2,1)S(1)}, u32[]{:S(2)}, u32[]{:S(2)}) %collective-permute-start.6) | collective-permute-done | bytes 98336 | tf_op jit(solution)/shard_map/ppermute | solution.py:426
  44.3 1.9 %shard_map.66 = bf16[32,112,256]{2,1,0:T(8,128)(2,1)} custom-call(bf16[192,256]{1,0:T(8,128)(2,1)S(1)} %get-tuple-element.10.refs_0_, bf16[192,256]{1,0:T(8,128)(2,1)S(1)} %collective-permute-done.refs_1_, bf16[192,256]{1,0:T(8,128)(2,1)S(1)} %collective-permute-done.1.refs_2_, bf16[192,256]{1,0:T(8,128)(2,1)S(1)} %collective-permute-done.2.refs_3_, ...), custom_call_target="tpu_custom_call" | custom-call | tf_op jit(solution)/shard_map/pallas_call | solution.py:440
  46.2 5.3 %all-to-all-start.1 = ((bf16[32,112,256]{2,1,0:T(8,128)(2,1)}), bf16[32,112,256]{2,1,0:T(8,128)(2,1)S(1)}, u32[]{:S(2)}, u32[]{:S(2)}) async-start(bf16[32,112,256]{2,1,0:T(8,128)(2,1)} %shard_map.66), calls=%async_computation.1 | async-start | bytes 3670016 | tf_op jit(solution)/shard_map/all_to_all | solution.py:451
  51.6 24.4 %all-to-all-done.1.got_ref = bf16[32,112,256]{2,1,0:T(8,128)(2,1)S(1)} async-done(((bf16[32,112,256]{2,1,0:T(8,128)(2,1)}), bf16[32,112,256]{2,1,0:T(8,128)(2,1)S(1)}, u32[]{:S(2)}, u32[]{:S(2)}) %all-to-all-start.1) | async-done | bytes 1835040 | tf_op jit(solution)/shard_map/all_to_all | solution.py:451
  76.0 13.5 %shard_map.67 = (f32[256,256]{1,0:T(8,128)}, f32[5,128,128]{2,1,0:T(8,128)S(1)}) custom-call(s32[24]{0:T(128)S(1)} %copy-done, s32[1]{0:T(128)} %bitcast.base_ref, bf16[24,64,4096]{2,1,0:T(8,128)(2,1)} %tensor_ref.1, bf16[32,112,256]{2,1,0:T(8,128)(2,1)S(1)} %all-to-all-done.1.got_ref), custom_call_target="tpu_custom_call" | custom-call | flops 3221225472 | bytes 12582912 | tf_op jit(solution)/shard_map/pallas_call | solution.py:352
  89.6 3.6 %all-to-all-start.2 = ((f32[4,64,256]{2,1,0:T(8,128)}), f32[4,64,256]{2,1,0:T(8,128)S(1)}, u32[]{:S(2)}, u32[]{:S(2)}) async-start(f32[4,64,256]{2,1,0:T(8,128)} %bitcast.11), calls=%async_computation.2 | async-start | bytes 524288 | tf_op jit(solution)/shard_map/all_to_all | solution.py:454
  93.2 4.5 %shard_map.68.inverse_ref = f32[256,256]{1,0:T(8,128)S(1)} custom-call(f32[5,128,128]{2,1,0:T(8,128)S(1)} %get-tuple-element.14.state_ref), custom_call_target="tpu_custom_call" | custom-call | flops 1000000000 | bytes 1000000 | tf_op jit(solution)/shard_map/pallas_call | solution.py:455
  97.7 2.0 %all-to-all-done.2.parts_ref = f32[4,64,256]{2,1,0:T(8,128)S(1)} async-done(((f32[4,64,256]{2,1,0:T(8,128)}), f32[4,64,256]{2,1,0:T(8,128)S(1)}, u32[]{:S(2)}, u32[]{:S(2)}) %all-to-all-start.2) | async-done | bytes 262176 | tf_op jit(solution)/shard_map/all_to_all | solution.py:454
  99.7 1.4 %shard_map.69 = f32[64,256]{1,0:T(8,128)} custom-call(f32[4,64,256]{2,1,0:T(8,128)S(1)} %all-to-all-done.2.parts_ref, f32[256,256]{1,0:T(8,128)S(1)} %shard_map.68.inverse_ref), custom_call_target="tpu_custom_call" | custom-call | tf_op jit(solution)/shard_map/pallas_call | solution.py:461
  (26 shorter events, 0.3 us)
Async XLA Ops:
  2.3 10.9 %all-to-all-start = ((bf16[8,48,256]{2,1,0:T(8,128)(2,1)}), bf16[8,48,256]{2,1,0:T(8,128)(2,1)S(1)}, u32[]{:S(2)}, u32[]{:S(2)}) async-start(bf16[8,48,256]{2,1,0:T(8,128)(2,1)} %shard_map.64), calls=%async_computation | async-start | bytes 393216 | tf_op jit(solution)/shard_map/all_to_all | solution.py:412
  13.3 7.6 %collective-permute-start.3 = (bf16[192,256]{1,0:T(8,128)(2,1)S(1)}, bf16[192,256]{1,0:T(8,128)(2,1)S(1)}, u32[]{:S(2)}, u32[]{:S(2)}) collective-permute-start(bf16[192,256]{1,0:T(8,128)(2,1)S(1)} %get-tuple-element.10.refs_0_), channel_id=1, source_target_pairs={{0,56},{8,0},{16,8},{24,16},{32,24},{40,32},{48,40},{56,48},{1,57}... | collective-permute-start | bytes 294920 | tf_op jit(solution)/shard_map/ppermute | solution.py:425
  18.6 5.8 %collective-permute-start = (bf16[192,256]{1,0:T(8,128)(2,1)S(1)}, bf16[192,256]{1,0:T(8,128)(2,1)S(1)}, u32[]{:S(2)}, u32[]{:S(2)}) collective-permute-start(bf16[192,256]{1,0:T(8,128)(2,1)S(1)} %get-tuple-element.10.refs_0_), channel_id=1, source_target_pairs={{0,8},{8,16},{16,24},{24,32},{32,40},{40,48},{48,56},{56,0},{1,9},... | collective-permute-start | bytes 294920 | tf_op jit(solution)/shard_map/ppermute | solution.py:424
  20.8 5.8 %collective-permute-start.4 = (bf16[192,256]{1,0:T(8,128)(2,1)S(1)}, bf16[192,256]{1,0:T(8,128)(2,1)S(1)}, u32[]{:S(2)}, u32[]{:S(2)}) collective-permute-start(bf16[192,256]{1,0:T(8,128)(2,1)S(1)} %collective-permute-done.3.refs_4_), channel_id=1, source_target_pairs={{0,56},{8,0},{16,8},{24,16},{32,24},{40,32},{48,40},{56,48},{1,57}... | collective-permute-start | bytes 294920 | tf_op jit(solution)/shard_map/ppermute | solution.py:425
  24.5 10.9 %collective-permute-start.1 = (bf16[192,256]{1,0:T(8,128)(2,1)S(1)}, bf16[192,256]{1,0:T(8,128)(2,1)S(1)}, u32[]{:S(2)}, u32[]{:S(2)}) collective-permute-start(bf16[192,256]{1,0:T(8,128)(2,1)S(1)} %collective-permute-done.refs_1_), channel_id=1, source_target_pairs={{0,8},{8,16},{16,24},{24,32},{32,40},{40,48},{48,56},{56,0},{1,9},... | collective-permute-start | bytes 294920 | tf_op jit(solution)/shard_map/ppermute | solution.py:424
  26.7 8.7 %collective-permute-start.7 = (s32[16,128]{1,0:T(8,128)S(1)}, s32[16,128]{1,0:T(8,128)S(1)}, u32[]{:S(2)}, u32[]{:S(2)}) collective-permute-start(s32[16,128]{1,0:T(8,128)S(1)} %get-tuple-element.12), channel_id=1, source_target_pairs={{0,3},{1,0},{2,1},{3,2},{4,7},{5,4},{6,5},{7,6},{8,11},{9,8},{10,9... | collective-permute-start | bytes 24584 | tf_op jit(solution)/shard_map/ppermute | solution.py:430
  29.4 6.0 %collective-permute-start.9 = (s32[16,128]{1,0:T(8,128)S(1)}, s32[16,128]{1,0:T(8,128)S(1)}, u32[]{:S(2)}, u32[]{:S(2)}) collective-permute-start(s32[16,128]{1,0:T(8,128)S(1)} %get-tuple-element.12), channel_id=1, source_target_pairs={{0,1},{1,2},{2,3},{3,0},{4,5},{5,6},{6,7},{7,4},{8,9},{9,10},{10,1... | collective-permute-start | bytes 24584 | tf_op jit(solution)/shard_map/ppermute | solution.py:430
  29.4 5.9 %collective-permute-start.8 = (s32[16,128]{1,0:T(8,128)S(1)}, s32[16,128]{1,0:T(8,128)S(1)}, u32[]{:S(2)}, u32[]{:S(2)}) collective-permute-start(s32[16,128]{1,0:T(8,128)S(1)} %get-tuple-element.12), channel_id=1, source_target_pairs={{0,2},{1,3},{2,0},{3,1},{4,6},{5,7},{6,4},{7,5},{8,10},{9,11},{10,... | collective-permute-start | bytes 24584 | tf_op jit(solution)/shard_map/ppermute | solution.py:430
  31.7 6.7 %collective-permute-start.5 = (bf16[192,256]{1,0:T(8,128)(2,1)S(1)}, bf16[192,256]{1,0:T(8,128)(2,1)S(1)}, u32[]{:S(2)}, u32[]{:S(2)}) collective-permute-start(bf16[192,256]{1,0:T(8,128)(2,1)S(1)} %collective-permute-done.4.refs_5_), channel_id=1, source_target_pairs={{0,56},{8,0},{16,8},{24,16},{32,24},{40,32},{48,40},{56,48},{1,57}... | collective-permute-start | bytes 294920 | tf_op jit(solution)/shard_map/ppermute | solution.py:425
  35.3 6.9 %collective-permute-start.2 = (bf16[192,256]{1,0:T(8,128)(2,1)S(1)}, bf16[192,256]{1,0:T(8,128)(2,1)S(1)}, u32[]{:S(2)}, u32[]{:S(2)}) collective-permute-start(bf16[192,256]{1,0:T(8,128)(2,1)S(1)} %collective-permute-done.1.refs_2_), channel_id=1, source_target_pairs={{0,8},{8,16},{16,24},{24,32},{32,40},{40,48},{48,56},{56,0},{1,9},... | collective-permute-start | bytes 294920 | tf_op jit(solution)/shard_map/ppermute | solution.py:424
  38.4 5.9 %collective-permute-start.6 = (bf16[192,256]{1,0:T(8,128)(2,1)S(1)}, bf16[192,256]{1,0:T(8,128)(2,1)S(1)}, u32[]{:S(2)}, u32[]{:S(2)}) collective-permute-start(bf16[192,256]{1,0:T(8,128)(2,1)S(1)} %collective-permute-done.5.refs_6_), channel_id=1, source_target_pairs={{0,56},{8,0},{16,8},{24,16},{32,24},{40,32},{48,40},{56,48},{1,57}... | collective-permute-start | bytes 294920 | tf_op jit(solution)/shard_map/ppermute | solution.py:426
  46.2 29.8 %copy-start = (s32[24]{0:T(128)S(1)}, s32[24]{0:T(128)}, u32[]{:S(2)}) copy-start(s32[24]{0:T(128)} %rows_ref.1) | copy-start | bytes 292
  46.2 29.8 %all-to-all-start.1 = ((bf16[32,112,256]{2,1,0:T(8,128)(2,1)}), bf16[32,112,256]{2,1,0:T(8,128)(2,1)S(1)}, u32[]{:S(2)}, u32[]{:S(2)}) async-start(bf16[32,112,256]{2,1,0:T(8,128)(2,1)} %shard_map.66), calls=%async_computation.1 | async-start | bytes 3670016 | tf_op jit(solution)/shard_map/all_to_all | solution.py:451
  89.6 10.1 %all-to-all-start.2 = ((f32[4,64,256]{2,1,0:T(8,128)}), f32[4,64,256]{2,1,0:T(8,128)S(1)}, u32[]{:S(2)}, u32[]{:S(2)}) async-start(f32[4,64,256]{2,1,0:T(8,128)} %bitcast.11), calls=%async_computation.2 | async-start | bytes 524288 | tf_op jit(solution)/shard_map/all_to_all | solution.py:454

commit v5 on v4

--- a/solution.py
+++ b/solution.py
@@ -297,7 +297,9 @@
     return upper, below, corner, scales[0][1], scales[1][1]
 
 
-def product_kernel(rows_ref, base_ref, tensor_ref, got_ref, out_ref, state_ref, wide, blocks, sems):
+def product_kernel(rows_ref, base_ref, x_ref, tensor_ref, got_ref, *refs):
+    out_refs, (state_ref, out_ref, wide, blocks, sems) = refs[:XS], refs[XS:]
+
     def fetch(t):
         return pltpu.make_async_copy(tensor_ref.at[t], blocks.at[t], sems.at[t])
 
@@ -328,17 +330,19 @@
                 jnp.concatenate(parts, axis=0),
                 preferred_element_type=F32,
             )
-        place = pl.multiple_of((rows_ref[t] - base_ref[0]) * BS, BS)
+        place = pl.multiple_of(((rows_ref[t] - base_ref[0] - x_ref[0]) & (XS - 1)) * BS, BS)
         out_ref[pl.ds(place, BS), :] += total
 
     taken = 0
     for t in range(BLK):
-        for later in range(t, {0: 4, 4: 12, 12: BLK}.get(t, t)):
+        for later in range(t, {0: 2, 2: 8, 8: BLK}.get(t, t)):
             fetch(later).wait()
         one_block(t)
         while taken < min(half // 8, (t + 1) * half // 8 // (BLK - 4)):
             next(steps)
             taken += 1
+    for n in range(XS):
+        out_refs[n][...] = out_ref[BS * n : BS * (n + 1), :]
     first = finish(steps)
     lower = dot_high(below, first, ((1,), (1,)))
     state_ref[0] = first
@@ -348,15 +352,16 @@
     state_ref[4] = jnp.broadcast_to(scale_last, (half, half))
 
 
-def products(block_rows, base, tensor_blocks, got):
+def products(block_rows, base, x, tensor_blocks, got):
     return call(
         product_kernel,
         (
-            jax.ShapeDtypeStruct((XS * BS, R), F32),
+            *[jax.ShapeDtypeStruct((BS, R), F32)] * XS,
             jax.ShapeDtypeStruct((5, R // 2, R // 2), F32),
         ),
-        [SMEM, SMEM, HBM, VMEM],
+        [SMEM, SMEM, SMEM, HBM, VMEM],
         [
+            pltpu.VMEM((XS * BS, R), F32),
             halves(PEERS * ROWS2),
             pltpu.VMEM((BLK, BS, BS * BS), BF16),
             pltpu.SemaphoreType.DMA((BLK,)),
@@ -364,7 +369,7 @@
         cost_estimate=pl.CostEstimate(
             flops=2 * BLK * BS * BS * BS * R, bytes_accessed=BLK * BS * BS * BS * 2, transcendentals=0
         ),
-    )(block_rows, base, tensor_blocks, got)
+    )(block_rows, base, x, tensor_blocks, got)
 
 
 def inverse_kernel(state_ref, out_ref):
@@ -381,8 +386,9 @@
     out_ref[half:, half:] = last * scale_last
 
 
-def final_kernel(parts_ref, inverse_ref, out_ref):
-    rows = (parts_ref[0] + parts_ref[1]) + (parts_ref[2] + parts_ref[3])
+def final_kernel(*refs):
+    parts, (inverse_ref, out_ref) = [ref[...] for ref in refs[:XS]], refs[XS:]
+    rows = (parts[0] + parts[1]) + (parts[2] + parts[3])
     inverse = inverse_ref[...]
     halfway = dot_high(rows, inverse, ((1,), (1,)))
     out_ref[...] = dot_high(halfway, inverse)
@@ -450,15 +456,17 @@
     )(*pieces, one_hot(place_two, 64 * ZS), one_hot(place_three, 32 * ZS), one_hot(place_three + PAIRS, 32 * ZS))
     got2 = exchange(sent, RING)
 
-    summed, state = products(block_rows, base, tensor_blocks, got2)
-    parts = exchange(summed.reshape(XS, BS, R), "x")
+    *summed, state = products(block_rows, base, x, tensor_blocks, got2)
+    parts = [summed[0]] + [
+        lax.ppermute(summed[step], "x", [(n, (n + step) % XS) for n in range(XS)]) for step in (1, 2, 3)
+    ]
     inverse = call(
         inverse_kernel,
         shape((R, R), F32),
         [VMEM],
         cost_estimate=pl.CostEstimate(flops=10**9, bytes_accessed=10**6, transcendentals=0),
     )(state)
-    return call(final_kernel, shape((BS, R), F32), [VMEM] * 2)(parts, inverse)
+    return call(final_kernel, shape((BS, R), F32), [VMEM] * (XS + 1))(*parts, inverse)
 
 
 def solution(mesh):

time: 101 us -> 101 us (level); the launches traced: 101 us -> 99.2 us
  waiting for transfers between devices: 40.7 us -> 38.7 us
    ppermute x0 -> x3, starting transfers between devices: none -> 4.08 us  [body(): lax.ppermute(summed[step], 'x', [(n, (n + step) % XS) for n in range(XS)])]
    all_to_all x1 -> x0, starting transfers between devices: 3.64 us -> none  [body(): parts = exchange(summed.reshape(XS, BS, R), 'x')]
    all_to_all x1 -> x0, waiting for transfers between devices: 1.97 us -> none  [body(): parts = exchange(summed.reshape(XS, BS, R), 'x')]
  transfers between devices with their start and end apart: 13 -> 15, of which waited for: 7 -> 6; matrix products, arithmetic and copies ran while one was open for 1% -> 1% of each run, Pallas kernels for 4% -> 5%
where the time goes in v5:
time: 101 us; the launch traced here: 99.2 us
  waiting for transfers between devices  38.7 us (38%)
  starting transfers between devices  36.2 us (36%)
  Pallas kernels  23.4 us (23%)
    all_to_all x1, waiting for transfers between devices, body(): got2 = exchange(sent, RING)  24.4 us
    pallas_call x1, Pallas kernels, products(): call(product_kernel, (*[jax.ShapeDtypeStruct((BS, R), F32)] * XS, jax.Sha...  13.2 us
    ppermute x3, starting transfers between devices, body(): from_high.append(lax.ppermute(from_high[-1], 'z', around[1]))  12.6 us
    ppermute x3, waiting for transfers between devices, body(): from_high.append(lax.ppermute(from_high[-1], 'z', around[1]))  6.82 us
    all_to_all x1, starting transfers between devices, body(): got0 = exchange(sent, ('y', 'c'))  5.5 us
    all_to_all x1, waiting for transfers between devices, body(): got0 = exchange(sent, ('y', 'c'))  5.41 us
    all_to_all x1, starting transfers between devices, body(): got2 = exchange(sent, RING)  5.32 us
    ppermute x3, starting transfers between devices, body(): lax.ppermute(places, 'x', [(n, (n + step) % XS) for n in range(XS)])  5.05 us
  transfers between devices with their start and end apart: 15, of which 6 were waited for; matrix products, arithmetic and copies ran while one was open for 1% of the time, Pallas kernels for 5%

profile of v5, /device:TPU:8, one launch (start us, length us, event | category | flops | bytes accessed | tf_op | source)
XLA Modules:
  0.0 99.2 jit_solution(14162827384722873940)
XLA Ops:
  0.0 2.3 %shard_map.64 = bf16[8,48,256]{2,1,0:T(8,128)(2,1)} custom-call(s32[1]{0:T(128)} %bitcast.1.x_ref, bf16[512,256]{1,0:T(8,128)(2,1)} %second_ref.1, bf16[128,256]{1,0:T(8,128)(2,1)} %third_ref.1, s32[1,24]{1,0:T(1,128)} %bitcast.21, s32[1,24]{1,0:T(1,128)} %bitcast.22), custom_call_target="tpu_custom_call" | custom-call | tf_op jit(solution)/shard_map/pallas_call | solution.py:405
  2.3 5.5 %all-to-all-start = ((bf16[8,48,256]{2,1,0:T(8,128)(2,1)}), bf16[8,48,256]{2,1,0:T(8,128)(2,1)S(1)}, u32[]{:S(2)}, u32[]{:S(2)}) async-start(bf16[8,48,256]{2,1,0:T(8,128)(2,1)} %shard_map.64), calls=%async_computation | async-start | bytes 393216 | tf_op jit(solution)/shard_map/all_to_all | solution.py:418
  7.8 5.4 %all-to-all-done.got_ref = bf16[8,48,256]{2,1,0:T(8,128)(2,1)S(1)} async-done(((bf16[8,48,256]{2,1,0:T(8,128)(2,1)}), bf16[8,48,256]{2,1,0:T(8,128)(2,1)S(1)}, u32[]{:S(2)}, u32[]{:S(2)}) %all-to-all-start) | async-done | bytes 196640 | tf_op jit(solution)/shard_map/all_to_all | solution.py:418
  13.2 0.1 shard_map.65
  13.3 5.3 %collective-permute-start.3 = (bf16[192,256]{1,0:T(8,128)(2,1)S(1)}, bf16[192,256]{1,0:T(8,128)(2,1)S(1)}, u32[]{:S(2)}, u32[]{:S(2)}) collective-permute-start(bf16[192,256]{1,0:T(8,128)(2,1)S(1)} %get-tuple-element.13.refs_0_), channel_id=1, source_target_pairs={{0,56},{8,0},{16,8},{24,16},{32,24},{40,32},{48,40},{56,48},{1,57}... | collective-permute-start | bytes 294920 | tf_op jit(solution)/shard_map/ppermute | solution.py:431
  18.6 2.2 %collective-permute-done.3.refs_4_ = bf16[192,256]{1,0:T(8,128)(2,1)S(1)} collective-permute-done((bf16[192,256]{1,0:T(8,128)(2,1)S(1)}, bf16[192,256]{1,0:T(8,128)(2,1)S(1)}, u32[]{:S(2)}, u32[]{:S(2)}) %collective-permute-start.3) | collective-permute-done | bytes 98336 | tf_op jit(solution)/shard_map/ppermute | solution.py:431
  20.8 3.6 %collective-permute-start.4 = (bf16[192,256]{1,0:T(8,128)(2,1)S(1)}, bf16[192,256]{1,0:T(8,128)(2,1)S(1)}, u32[]{:S(2)}, u32[]{:S(2)}) collective-permute-start(bf16[192,256]{1,0:T(8,128)(2,1)S(1)} %collective-permute-done.3.refs_4_), channel_id=1, source_target_pairs={{0,56},{8,0},{16,8},{24,16},{32,24},{40,32},{48,40},{56,48},{1,57}... | collective-permute-start | bytes 294920 | tf_op jit(solution)/shard_map/ppermute | solution.py:431
  24.5 2.2 %collective-permute-done.4.refs_5_ = bf16[192,256]{1,0:T(8,128)(2,1)S(1)} collective-permute-done((bf16[192,256]{1,0:T(8,128)(2,1)S(1)}, bf16[192,256]{1,0:T(8,128)(2,1)S(1)}, u32[]{:S(2)}, u32[]{:S(2)}) %collective-permute-start.4) | collective-permute-done | bytes 98336 | tf_op jit(solution)/shard_map/ppermute | solution.py:431
  26.7 2.8 %collective-permute-start.7 = (s32[16,128]{1,0:T(8,128)S(1)}, s32[16,128]{1,0:T(8,128)S(1)}, u32[]{:S(2)}, u32[]{:S(2)}) collective-permute-start(s32[16,128]{1,0:T(8,128)S(1)} %get-tuple-element.15), channel_id=1, source_target_pairs={{0,3},{1,0},{2,1},{3,2},{4,7},{5,4},{6,5},{7,6},{8,11},{9,8},{10,9... | collective-permute-start | bytes 24584 | tf_op jit(solution)/shard_map/ppermute | solution.py:436
  29.4 2.3 %collective-permute-start.8 = (s32[16,128]{1,0:T(8,128)S(1)}, s32[16,128]{1,0:T(8,128)S(1)}, u32[]{:S(2)}, u32[]{:S(2)}) collective-permute-start(s32[16,128]{1,0:T(8,128)S(1)} %get-tuple-element.15), channel_id=1, source_target_pairs={{0,2},{1,3},{2,0},{3,1},{4,6},{5,7},{6,4},{7,5},{8,10},{9,11},{10,... | collective-permute-start | bytes 24584 | tf_op jit(solution)/shard_map/ppermute | solution.py:436
  31.7 3.6 %collective-permute-start.5 = (bf16[192,256]{1,0:T(8,128)(2,1)S(1)}, bf16[192,256]{1,0:T(8,128)(2,1)S(1)}, u32[]{:S(2)}, u32[]{:S(2)}) collective-permute-start(bf16[192,256]{1,0:T(8,128)(2,1)S(1)} %collective-permute-done.4.refs_5_), channel_id=1, source_target_pairs={{0,56},{8,0},{16,8},{24,16},{32,24},{40,32},{48,40},{56,48},{1,57}... | collective-permute-start | bytes 294920 | tf_op jit(solution)/shard_map/ppermute | solution.py:431
  35.6 0.3 fusion.1
  36.0 2.4 %collective-permute-done.5.refs_6_ = bf16[192,256]{1,0:T(8,128)(2,1)S(1)} collective-permute-done((bf16[192,256]{1,0:T(8,128)(2,1)S(1)}, bf16[192,256]{1,0:T(8,128)(2,1)S(1)}, u32[]{:S(2)}, u32[]{:S(2)}) %collective-permute-start.5) | collective-permute-done | bytes 98336 | tf_op jit(solution)/shard_map/ppermute | solution.py:431
  38.4 3.7 %collective-permute-start.6 = (bf16[192,256]{1,0:T(8,128)(2,1)S(1)}, bf16[192,256]{1,0:T(8,128)(2,1)S(1)}, u32[]{:S(2)}, u32[]{:S(2)}) collective-permute-start(bf16[192,256]{1,0:T(8,128)(2,1)S(1)} %collective-permute-done.5.refs_6_), channel_id=1, source_target_pairs={{0,56},{8,0},{16,8},{24,16},{32,24},{40,32},{48,40},{56,48},{1,57}... | collective-permute-start | bytes 294920 | tf_op jit(solution)/shard_map/ppermute | solution.py:432
  42.1 0.2 fusion.refs_8_
  42.3 2.0 %collective-permute-done.6.refs_7_ = bf16[192,256]{1,0:T(8,128)(2,1)S(1)} collective-permute-done((bf16[192,256]{1,0:T(8,128)(2,1)S(1)}, bf16[192,256]{1,0:T(8,128)(2,1)S(1)}, u32[]{:S(2)}, u32[]{:S(2)}) %collective-permute-start.6) | collective-permute-done | bytes 98336 | tf_op jit(solution)/shard_map/ppermute | solution.py:432
  44.3 1.9 %shard_map.66 = bf16[32,112,256]{2,1,0:T(8,128)(2,1)} custom-call(bf16[192,256]{1,0:T(8,128)(2,1)S(1)} %get-tuple-element.13.refs_0_, bf16[192,256]{1,0:T(8,128)(2,1)S(1)} %collective-permute-done.refs_1_, bf16[192,256]{1,0:T(8,128)(2,1)S(1)} %collective-permute-done.1.refs_2_, bf16[192,256]{1,0:T(8,128)(2,1)S(1)} %collective-permute-done.2.refs_3_, ...), custom_call_target="tpu_custom_call" | custom-call | tf_op jit(solution)/shard_map/pallas_call | solution.py:446
  46.2 5.3 %all-to-all-start.1 = ((bf16[32,112,256]{2,1,0:T(8,128)(2,1)}), bf16[32,112,256]{2,1,0:T(8,128)(2,1)S(1)}, u32[]{:S(2)}, u32[]{:S(2)}) async-start(bf16[32,112,256]{2,1,0:T(8,128)(2,1)} %shard_map.66), calls=%async_computation.1 | async-start | bytes 3670016 | tf_op jit(solution)/shard_map/all_to_all | solution.py:457
  51.6 24.4 %all-to-all-done.1.got_ref = bf16[32,112,256]{2,1,0:T(8,128)(2,1)S(1)} async-done(((bf16[32,112,256]{2,1,0:T(8,128)(2,1)}), bf16[32,112,256]{2,1,0:T(8,128)(2,1)S(1)}, u32[]{:S(2)}, u32[]{:S(2)}) %all-to-all-start.1) | async-done | bytes 1835040 | tf_op jit(solution)/shard_map/all_to_all | solution.py:457
  76.0 13.2 %shard_map.67 = (f32[64,256]{1,0:T(8,128)S(1)}, f32[64,256]{1,0:T(8,128)S(1)}, f32[64,256]{1,0:T(8,128)S(1)}, f32[64,256]{1,0:T(8,128)S(1)}, f32[5,128,128]{2,1,0:T(8,128)S(1)}) custom-call(s32[24]{0:T(128)S(1)} %copy-done, s32[1]{0:T(128)} %bitcast.base_ref, s32[1]{0:T(128)} %bitcast.1.x_ref, bf16[24,64,4096]{2,1,0:T(8,128)(2,1)} %tensor_ref.1, ...), custom_call_target="tpu_custom_call" | custom-call | flops 3221225472 | bytes 12582912 | tf_op jit(solution)/shard_map/pallas_call | solution.py:356
  89.3 2.5 %collective-permute-start.11 = (f32[64,256]{1,0:T(8,128)S(1)}, f32[64,256]{1,0:T(8,128)S(1)}, u32[]{:S(2)}, u32[]{:S(2)}) collective-permute-start(f32[64,256]{1,0:T(8,128)S(1)} %get-tuple-element.18), channel_id=1, source_target_pairs={{0,2},{1,3},{2,0},{3,1},{4,6},{5,7},{6,4},{7,5},{8,10},{9,11},{10,... | collective-permute-start | bytes 196616 | tf_op jit(solution)/shard_map/ppermute | solution.py:461
  91.8 1.5 %collective-permute-start.12 = (f32[64,256]{1,0:T(8,128)S(1)}, f32[64,256]{1,0:T(8,128)S(1)}, u32[]{:S(2)}, u32[]{:S(2)}) collective-permute-start(f32[64,256]{1,0:T(8,128)S(1)} %get-tuple-element.19), channel_id=1, source_target_pairs={{0,3},{1,0},{2,1},{3,2},{4,7},{5,4},{6,5},{7,6},{8,11},{9,8},{10,9... | collective-permute-start | bytes 196616 | tf_op jit(solution)/shard_map/ppermute | solution.py:461
  93.3 4.5 %shard_map.68.refs_4_ = f32[256,256]{1,0:T(8,128)S(1)} custom-call(f32[5,128,128]{2,1,0:T(8,128)S(1)} %get-tuple-element.20.state_ref), custom_call_target="tpu_custom_call" | custom-call | flops 1000000000 | bytes 1000000 | tf_op jit(solution)/shard_map/pallas_call | solution.py:463
  97.8 1.4 %shard_map.69 = f32[64,256]{1,0:T(8,128)} custom-call(f32[64,256]{1,0:T(8,128)S(1)} %get-tuple-element.16.refs_0_, f32[64,256]{1,0:T(8,128)S(1)} %collective-permute-done.10.refs_1_, f32[64,256]{1,0:T(8,128)S(1)} %collective-permute-done.11.refs_2_, f32[64,256]{1,0:T(8,128)S(1)} %collective-permute-done.12.refs_3_, f32[256,256]{1,0:T(8,128)S(1)} %shard_map.68.refs_4_), custom_call_target="tpu_custom_call" | custom-call | tf_op jit(solution)/shard_map/pallas_call | solution.py:469
  (30 shorter events, 0.4 us)
Async XLA Ops:
  2.3 10.9 %all-to-all-start = ((bf16[8,48,256]{2,1,0:T(8,128)(2,1)}), bf16[8,48,256]{2,1,0:T(8,128)(2,1)S(1)}, u32[]{:S(2)}, u32[]{:S(2)}) async-start(bf16[8,48,256]{2,1,0:T(8,128)(2,1)} %shard_map.64), calls=%async_computation | async-start | bytes 393216 | tf_op jit(solution)/shard_map/all_to_all | solution.py:418
  13.3 7.6 %collective-permute-start.3 = (bf16[192,256]{1,0:T(8,128)(2,1)S(1)}, bf16[192,256]{1,0:T(8,128)(2,1)S(1)}, u32[]{:S(2)}, u32[]{:S(2)}) collective-permute-start(bf16[192,256]{1,0:T(8,128)(2,1)S(1)} %get-tuple-element.13.refs_0_), channel_id=1, source_target_pairs={{0,56},{8,0},{16,8},{24,16},{32,24},{40,32},{48,40},{56,48},{1,57}... | collective-permute-start | bytes 294920 | tf_op jit(solution)/shard_map/ppermute | solution.py:431
  18.6 5.8 %collective-permute-start = (bf16[192,256]{1,0:T(8,128)(2,1)S(1)}, bf16[192,256]{1,0:T(8,128)(2,1)S(1)}, u32[]{:S(2)}, u32[]{:S(2)}) collective-permute-start(bf16[192,256]{1,0:T(8,128)(2,1)S(1)} %get-tuple-element.13.refs_0_), channel_id=1, source_target_pairs={{0,8},{8,16},{16,24},{24,32},{32,40},{40,48},{48,56},{56,0},{1,9},... | collective-permute-start | bytes 294920 | tf_op jit(solution)/shard_map/ppermute | solution.py:430
  20.8 5.8 %collective-permute-start.4 = (bf16[192,256]{1,0:T(8,128)(2,1)S(1)}, bf16[192,256]{1,0:T(8,128)(2,1)S(1)}, u32[]{:S(2)}, u32[]{:S(2)}) collective-permute-start(bf16[192,256]{1,0:T(8,128)(2,1)S(1)} %collective-permute-done.3.refs_4_), channel_id=1, source_target_pairs={{0,56},{8,0},{16,8},{24,16},{32,24},{40,32},{48,40},{56,48},{1,57}... | collective-permute-start | bytes 294920 | tf_op jit(solution)/shard_map/ppermute | solution.py:431
  24.4 10.9 %collective-permute-start.1 = (bf16[192,256]{1,0:T(8,128)(2,1)S(1)}, bf16[192,256]{1,0:T(8,128)(2,1)S(1)}, u32[]{:S(2)}, u32[]{:S(2)}) collective-permute-start(bf16[192,256]{1,0:T(8,128)(2,1)S(1)} %collective-permute-done.refs_1_), channel_id=1, source_target_pairs={{0,8},{8,16},{16,24},{24,32},{32,40},{40,48},{48,56},{56,0},{1,9},... | collective-permute-start | bytes 294920 | tf_op jit(solution)/shard_map/ppermute | solution.py:430
  26.7 8.7 %collective-permute-start.7 = (s32[16,128]{1,0:T(8,128)S(1)}, s32[16,128]{1,0:T(8,128)S(1)}, u32[]{:S(2)}, u32[]{:S(2)}) collective-permute-start(s32[16,128]{1,0:T(8,128)S(1)} %get-tuple-element.15), channel_id=1, source_target_pairs={{0,3},{1,0},{2,1},{3,2},{4,7},{5,4},{6,5},{7,6},{8,11},{9,8},{10,9... | collective-permute-start | bytes 24584 | tf_op jit(solution)/shard_map/ppermute | solution.py:436
  29.4 6.0 %collective-permute-start.9 = (s32[16,128]{1,0:T(8,128)S(1)}, s32[16,128]{1,0:T(8,128)S(1)}, u32[]{:S(2)}, u32[]{:S(2)}) collective-permute-start(s32[16,128]{1,0:T(8,128)S(1)} %get-tuple-element.15), channel_id=1, source_target_pairs={{0,1},{1,2},{2,3},{3,0},{4,5},{5,6},{6,7},{7,4},{8,9},{9,10},{10,1... | collective-permute-start | bytes 24584 | tf_op jit(solution)/shard_map/ppermute | solution.py:436
  29.4 5.9 %collective-permute-start.8 = (s32[16,128]{1,0:T(8,128)S(1)}, s32[16,128]{1,0:T(8,128)S(1)}, u32[]{:S(2)}, u32[]{:S(2)}) collective-permute-start(s32[16,128]{1,0:T(8,128)S(1)} %get-tuple-element.15), channel_id=1, source_target_pairs={{0,2},{1,3},{2,0},{3,1},{4,6},{5,7},{6,4},{7,5},{8,10},{9,11},{10,... | collective-permute-start | bytes 24584 | tf_op jit(solution)/shard_map/ppermute | solution.py:436
  31.7 6.7 %collective-permute-start.5 = (bf16[192,256]{1,0:T(8,128)(2,1)S(1)}, bf16[192,256]{1,0:T(8,128)(2,1)S(1)}, u32[]{:S(2)}, u32[]{:S(2)}) collective-permute-start(bf16[192,256]{1,0:T(8,128)(2,1)S(1)} %collective-permute-done.4.refs_5_), channel_id=1, source_target_pairs={{0,56},{8,0},{16,8},{24,16},{32,24},{40,32},{48,40},{56,48},{1,57}... | collective-permute-start | bytes 294920 | tf_op jit(solution)/shard_map/ppermute | solution.py:431
  35.3 6.9 %collective-permute-start.2 = (bf16[192,256]{1,0:T(8,128)(2,1)S(1)}, bf16[192,256]{1,0:T(8,128)(2,1)S(1)}, u32[]{:S(2)}, u32[]{:S(2)}) collective-permute-start(bf16[192,256]{1,0:T(8,128)(2,1)S(1)} %collective-permute-done.1.refs_2_), channel_id=1, source_target_pairs={{0,8},{8,16},{16,24},{24,32},{32,40},{40,48},{48,56},{56,0},{1,9},... | collective-permute-start | bytes 294920 | tf_op jit(solution)/shard_map/ppermute | solution.py:430
  38.4 5.9 %collective-permute-start.6 = (bf16[192,256]{1,0:T(8,128)(2,1)S(1)}, bf16[192,256]{1,0:T(8,128)(2,1)S(1)}, u32[]{:S(2)}, u32[]{:S(2)}) collective-permute-start(bf16[192,256]{1,0:T(8,128)(2,1)S(1)} %collective-permute-done.5.refs_6_), channel_id=1, source_target_pairs={{0,56},{8,0},{16,8},{24,16},{32,24},{40,32},{48,40},{56,48},{1,57}... | collective-permute-start | bytes 294920 | tf_op jit(solution)/shard_map/ppermute | solution.py:432
  46.2 29.8 %copy-start = (s32[24]{0:T(128)S(1)}, s32[24]{0:T(128)}, u32[]{:S(2)}) copy-start(s32[24]{0:T(128)} %rows_ref.1) | copy-start | bytes 292
  46.2 29.8 %all-to-all-start.1 = ((bf16[32,112,256]{2,1,0:T(8,128)(2,1)}), bf16[32,112,256]{2,1,0:T(8,128)(2,1)S(1)}, u32[]{:S(2)}, u32[]{:S(2)}) async-start(bf16[32,112,256]{2,1,0:T(8,128)(2,1)} %shard_map.66), calls=%async_computation.1 | async-start | bytes 3670016 | tf_op jit(solution)/shard_map/all_to_all | solution.py:457
  89.2 8.6 %collective-permute-start.10 = (f32[64,256]{1,0:T(8,128)S(1)}, f32[64,256]{1,0:T(8,128)S(1)}, u32[]{:S(2)}, u32[]{:S(2)}) collective-permute-start(f32[64,256]{1,0:T(8,128)S(1)} %get-tuple-element.17), channel_id=1, source_target_pairs={{0,1},{1,2},{2,3},{3,0},{4,5},{5,6},{6,7},{7,4},{8,9},{9,10},{10,1... | collective-permute-start | bytes 196616 | tf_op jit(solution)/shard_map/ppermute | solution.py:461
  89.3 8.5 %collective-permute-start.11 = (f32[64,256]{1,0:T(8,128)S(1)}, f32[64,256]{1,0:T(8,128)S(1)}, u32[]{:S(2)}, u32[]{:S(2)}) collective-permute-start(f32[64,256]{1,0:T(8,128)S(1)} %get-tuple-element.18), channel_id=1, source_target_pairs={{0,2},{1,3},{2,0},{3,1},{4,6},{5,7},{6,4},{7,5},{8,10},{9,11},{10,... | collective-permute-start | bytes 196616 | tf_op jit(solution)/shard_map/ppermute | solution.py:461
  91.8 6.0 %collective-permute-start.12 = (f32[64,256]{1,0:T(8,128)S(1)}, f32[64,256]{1,0:T(8,128)S(1)}, u32[]{:S(2)}, u32[]{:S(2)}) collective-permute-start(f32[64,256]{1,0:T(8,128)S(1)} %get-tuple-element.19), channel_id=1, source_target_pairs={{0,3},{1,0},{2,1},{3,2},{4,7},{5,4},{6,5},{7,6},{8,11},{9,8},{10,9... | collective-permute-start | bytes 196616 | tf_op jit(solution)/shard_map/ppermute | solution.py:461
